TPU v7x, 32 devices: a whole 2x2x4 slice. The times are simulated.
32 devices in a mesh: dp: 4 (over x, core), seq: 8 (over z, y).
Axes of the slice: x: 2, y: 2, z: 4, core: 2. Of those that a mesh axis runs over, the one named last changes fastest.
Arguments:
- inputs: bfloat16 [2, 4, 1024, 768], P(None, 'dp', 'seq'), may hold values from -6 to 6
- cotangent: bfloat16 [2, 4, 1024, 768], P(None, 'dp', 'seq'), may hold values from -6 to 6
- live: int32 [2, 4], P(None, 'dp'), may hold values from 0 to 1, as said below
- first_qkv: bfloat16 [768, 2304], P('dp'), may hold values from -1 to 1
- first_out: bfloat16 [768, 768], P('dp'), may hold values from -4 to 4
- first_gain_a: bfloat16 [768], P('dp'), may hold values from 0.099609375 to 1.8984375
- first_shift_a: bfloat16 [768], P('dp'), may hold values from -3 to 3
- first_gate: bfloat16 [768, 3072], P('dp'), may hold values from -0.21875 to 0.21875
- first_up: bfloat16 [768, 3072], P('dp'), may hold values from -0.21875 to 0.21875
- first_down: bfloat16 [3072, 768], P('dp'), may hold values from -0.109375 to 0.109375
- first_gain_f: bfloat16 [768], P('dp'), may hold values from 0.099609375 to 1.8984375
- first_shift_f: bfloat16 [768], P('dp'), may hold values from -3 to 3
- second_qkv: bfloat16 [768, 2304], P('dp'), may hold values from -1 to 1
- second_out: bfloat16 [768, 768], P('dp'), may hold values from -4 to 4
- second_gain_a: bfloat16 [768], P('dp'), may hold values from 0.099609375 to 1.8984375
- second_shift_a: bfloat16 [768], P('dp'), may hold values from -3 to 3
- second_gate: bfloat16 [768, 3072], P('dp'), may hold values from -0.21875 to 0.21875
- second_up: bfloat16 [768, 3072], P('dp'), may hold values from -0.21875 to 0.21875
- second_down: bfloat16 [3072, 768], P('dp'), may hold values from -0.109375 to 0.109375
- second_gain_f: bfloat16 [768], P('dp'), may hold values from 0.099609375 to 1.8984375
- second_shift_f: bfloat16 [768], P('dp'), may hold values from -3 to 3
Outputs:
- output: bfloat16 [2, 4, 1024, 768], P(None, 'dp', 'seq')
- input_grad: bfloat16 [2, 4, 1024, 768], P(None, 'dp', 'seq')
- grad_first_qkv: float32 [768, 2304], P('dp')
- grad_first_out: float32 [768, 768], P('dp')
- grad_first_gain_a: float32 [768], P('dp')
- grad_first_shift_a: float32 [768], P('dp')
- grad_first_gate: float32 [768, 3072], P('dp')
- grad_first_up: float32 [768, 3072], P('dp')
- grad_first_down: float32 [3072, 768], P('dp')
- grad_first_gain_f: float32 [768], P('dp')
- grad_first_shift_f: float32 [768], P('dp')
- grad_second_qkv: float32 [768, 2304], P('dp')
- grad_second_out: float32 [768, 768], P('dp')
- grad_second_gain_a: float32 [768], P('dp')
- grad_second_shift_a: float32 [768], P('dp')
- grad_second_gate: float32 [768, 3072], P('dp')
- grad_second_up: float32 [768, 3072], P('dp')
- grad_second_down: float32 [3072, 768], P('dp')
- grad_second_gain_f: float32 [768], P('dp')
- grad_second_shift_f: float32 [768], P('dp')
Inputs may be any that keep to these rules, and one draw needn't show every extreme that they name: One micro-batch, drawn from the seed, has exactly one live slot, also drawn from the seed; every other micro-batch has every slot live.
All inputs are finite; a program needn't handle non-finite values.
Results may differ from a plain program's by a relative error of at most 0.028.
Values may be sent and summed in bfloat16 or wider, within the bound.
A program may use at most 512 MiB of HBM per device.

v0:
```python
import jax
import jax.numpy as jnp
from jax import lax
from jax.sharding import PartitionSpec as P

HEAD = 64


def as_sent(array):
    return jax.tree.map(lambda a: a.astype(jnp.bfloat16) if a.dtype == jnp.float32 else a, array)


def tables(positions):
    half = HEAD // 2
    freqs = 1000.0 ** (-(jnp.arange(half).astype(jnp.float32) * 2.0 / HEAD))
    angles = positions[:, None] * freqs[None, :]
    return (jnp.cos(angles), jnp.sin(angles))


def rotate(values, cosine, sine):
    half = HEAD // 2
    first = values[..., :half]
    second = values[..., half:]
    cos_b = cosine[:, None, :]
    sin_b = sine[:, None, :]
    return jnp.concatenate(
        [first * cos_b - second * sin_b, second * cos_b + first * sin_b], axis=-1
    )


def unrotate(values, cosine, sine):
    half = HEAD // 2
    first = values[..., :half]
    second = values[..., half:]
    cos_b = cosine[:, None, :]
    sin_b = sine[:, None, :]
    return jnp.concatenate(
        [first * cos_b + second * sin_b, second * cos_b - first * sin_b], axis=-1
    )


def layer_norm(rows, gain, shift):
    center = rows - jnp.mean(rows, axis=-1, keepdims=True)
    spread = jnp.mean(center * center, axis=-1, keepdims=True)
    return center * lax.rsqrt(spread + 1e-05) * gain + shift


def dot_first(left, right):
    return lax.dot_general(
        left, right, (((0,), (0,)), ((), ())), preferred_element_type=jnp.float32
    )


def dot_last(left, right):
    return lax.dot_general(
        left, right, (((1,), (1,)), ((), ())), preferred_element_type=jnp.float32
    )


def forward_layer(hidden_in, weights, cosine, sine):
    w_qkv, w_out, gain_a, shift_a, w_gate, w_up, w_down, gain_f, shift_f = weights
    tokens = hidden_in.shape[0]
    width = hidden_in.shape[1]
    heads = width // HEAD
    scale = HEAD ** (-0.5)
    act = hidden_in.astype(jnp.bfloat16)
    joint = jnp.dot(act, w_qkv, preferred_element_type=jnp.float32)
    query = joint[:, :width].reshape(tokens, heads, HEAD)
    keys = joint[:, width : 2 * width].reshape(tokens, heads, HEAD)
    query_r = rotate(query, cosine, sine).astype(jnp.bfloat16)
    keys_r = rotate(keys, cosine, sine).astype(jnp.bfloat16).reshape(tokens, width)
    values_r = joint[:, 2 * width :].astype(jnp.bfloat16)
    keys_all, values_all = (
        lax.all_gather(keys_r, "seq", axis=0, tiled=True),
        lax.all_gather(values_r, "seq", axis=0, tiled=True),
    )
    length = keys_all.shape[0]
    keys_all = keys_all.reshape(length, heads, HEAD)
    values_all = values_all.reshape(length, heads, HEAD)
    scores = (
        jnp.einsum("qhd,khd->hqk", query_r, keys_all, preferred_element_type=jnp.float32) * scale
    )
    top = jnp.max(scores, axis=-1, keepdims=True)
    expo = jnp.exp(scores - top)
    total = jnp.sum(expo, axis=-1, keepdims=True)
    probs = expo / total
    log_total = top + jnp.log(total)
    context = jnp.einsum(
        "hqk,khd->qhd", probs.astype(jnp.bfloat16), values_all, preferred_element_type=jnp.float32
    )
    context = context.reshape(tokens, width).astype(jnp.bfloat16)
    res_a = hidden_in + jnp.dot(context, w_out, preferred_element_type=jnp.float32)
    norm_a = layer_norm(res_a, gain_a.astype(jnp.float32), shift_a.astype(jnp.float32))
    act_f = norm_a.astype(jnp.bfloat16)
    gate_pre = jnp.dot(act_f, w_gate, preferred_element_type=jnp.float32)
    up_pre = jnp.dot(act_f, w_up, preferred_element_type=jnp.float32)
    hidden = (jax.nn.silu(gate_pre) * up_pre).astype(jnp.bfloat16)
    res_f = norm_a + jnp.dot(hidden, w_down, preferred_element_type=jnp.float32)
    result = layer_norm(res_f, gain_f.astype(jnp.float32), shift_f.astype(jnp.float32))
    saved = (
        act,
        query_r,
        keys_r,
        values_r,
        log_total,
        context,
        res_a,
        act_f,
        gate_pre,
        up_pre,
        hidden,
        res_f,
    )
    return (result, saved)


def backward_layer(grad_out, weights, saved, cosine, sine):
    w_qkv, w_out, gain_a, shift_a, w_gate, w_up, w_down, gain_f, shift_f = weights
    (
        act,
        query_r,
        keys_r,
        values_r,
        log_total,
        context,
        res_a,
        act_f,
        gate_pre,
        up_pre,
        hidden,
        res_f,
    ) = saved
    tokens = act.shape[0]
    width = act.shape[1]
    heads = width // HEAD
    scale = HEAD ** (-0.5)
    unused, pull_f = jax.vjp(
        layer_norm, res_f, gain_f.astype(jnp.float32), shift_f.astype(jnp.float32)
    )
    d_res_f, d_gain_f, d_shift_f = pull_f(grad_out)
    d_branch = d_res_f.astype(jnp.bfloat16)
    g_down = dot_first(hidden, d_branch)
    d_hidden = dot_last(d_branch, w_down)
    sigm = jax.nn.sigmoid(gate_pre)
    d_gate = (d_hidden * up_pre * sigm * (1.0 + gate_pre * (1.0 - sigm))).astype(jnp.bfloat16)
    d_up = (d_hidden * gate_pre * sigm).astype(jnp.bfloat16)
    g_gate = dot_first(act_f, d_gate)
    g_up = dot_first(act_f, d_up)
    d_norm_a = d_res_f + dot_last(d_gate, w_gate) + dot_last(d_up, w_up)
    unused, pull_a = jax.vjp(
        layer_norm, res_a, gain_a.astype(jnp.float32), shift_a.astype(jnp.float32)
    )
    d_res_a, d_gain_a, d_shift_a = pull_a(d_norm_a)
    d_attn = d_res_a.astype(jnp.bfloat16)
    g_out = dot_first(context, d_attn)
    d_context = dot_last(d_attn, w_out).astype(jnp.bfloat16).reshape(tokens, heads, HEAD)
    keys_all, values_all = (
        lax.all_gather(keys_r, "seq", axis=0, tiled=True),
        lax.all_gather(values_r, "seq", axis=0, tiled=True),
    )
    length = keys_all.shape[0]
    keys_all = keys_all.reshape(length, heads, HEAD)
    values_all = values_all.reshape(length, heads, HEAD)
    scores = (
        jnp.einsum("qhd,khd->hqk", query_r, keys_all, preferred_element_type=jnp.float32) * scale
    )
    probs = jnp.exp(scores - log_total)
    d_probs = jnp.einsum("qhd,khd->hqk", d_context, values_all, preferred_element_type=jnp.float32)
    inner = jnp.sum(probs * d_probs, axis=-1, keepdims=True)
    d_scores = (probs * (d_probs - inner)).astype(jnp.bfloat16)
    d_query = (
        jnp.einsum("hqk,khd->qhd", d_scores, keys_all, preferred_element_type=jnp.float32) * scale
    )
    d_keys_all = (
        jnp.einsum("hqk,qhd->khd", d_scores, query_r, preferred_element_type=jnp.float32) * scale
    )
    d_values_all = jnp.einsum(
        "hqk,qhd->khd", probs.astype(jnp.bfloat16), d_context, preferred_element_type=jnp.float32
    )
    d_keys, d_values = (
        lax.psum_scatter(
            d_keys_all.reshape(length, width).astype(jnp.bfloat16),
            "seq",
            scatter_dimension=0,
            tiled=True,
        ).astype(jnp.float32),
        lax.psum_scatter(
            d_values_all.reshape(length, width).astype(jnp.bfloat16),
            "seq",
            scatter_dimension=0,
            tiled=True,
        ).astype(jnp.float32),
    )
    d_query = unrotate(d_query, cosine, sine).reshape(tokens, width)
    d_keys = unrotate(d_keys.reshape(tokens, heads, HEAD), cosine, sine).reshape(tokens, width)
    d_joint = jnp.concatenate([d_query, d_keys, d_values], axis=1).astype(jnp.bfloat16)
    g_qkv = dot_first(act, d_joint)
    grad_in = d_res_a + dot_last(d_joint, w_qkv)
    return (grad_in, (g_qkv, g_out, d_gain_a, d_shift_a, g_gate, g_up, g_down, d_gain_f, d_shift_f))


def per_device(
    inputs,
    cotangent,
    live,
    first_qkv,
    first_out,
    first_gain_a,
    first_shift_a,
    first_gate,
    first_up,
    first_down,
    first_gain_f,
    first_shift_f,
    second_qkv,
    second_out,
    second_gain_a,
    second_shift_a,
    second_gate,
    second_up,
    second_down,
    second_gain_f,
    second_shift_f,
):
    local_sets = (
        (
            first_qkv,
            first_out,
            first_gain_a,
            first_shift_a,
            first_gate,
            first_up,
            first_down,
            first_gain_f,
            first_shift_f,
        ),
        (
            second_qkv,
            second_out,
            second_gain_a,
            second_shift_a,
            second_gate,
            second_up,
            second_down,
            second_gain_f,
            second_shift_f,
        ),
    )
    micro = inputs.shape[0]
    tokens = inputs.shape[2]
    groups = lax.axis_size("dp")
    positions = (lax.axis_index("seq") * tokens + jnp.arange(tokens)).astype(jnp.float32)
    cosine, sine = tables(positions)
    totals = [
        tuple(
            (jnp.zeros((w.shape[0] * groups,) + w.shape[1:], jnp.float32) for w in local_sets[0])
        ),
        tuple(
            (jnp.zeros((w.shape[0] * groups,) + w.shape[1:], jnp.float32) for w in local_sets[1])
        ),
    ]
    results = []
    grads_in = []
    for batch in range(micro):
        flag = live[batch, 0].astype(jnp.float32)
        state = inputs[batch, 0].astype(jnp.float32)
        held = []
        saves = []
        for index in range(2):
            full = lax.all_gather(as_sent(local_sets[index]), "dp", axis=0, tiled=True)
            held.append(full)
            state, saved = forward_layer(state, full, cosine, sine)
            saves.append(saved)
        results.append((state * flag).astype(jnp.bfloat16))
        grad = cotangent[batch, 0].astype(jnp.float32) * flag
        for index in (1, 0):
            full = lax.all_gather(as_sent(local_sets[index]), "dp", axis=0, tiled=True)
            grad, terms = backward_layer(grad, full, saves[index], cosine, sine)
            totals[index] = tuple((old + new for old, new in zip(totals[index], terms)))
        grads_in.append(grad.astype(jnp.bfloat16))
    summed = []
    for index in range(2):
        shares = jax.tree.map(
            lambda part: part.astype(jnp.float32),
            lax.psum_scatter(as_sent(totals[index]), "dp", scatter_dimension=0, tiled=True),
        )
        final = jax.tree.map(
            lambda part: part.astype(jnp.float32), lax.psum(as_sent(shares), "seq")
        )
        summed.extend(final)
    output = jnp.stack(results)[:, None]
    input_grad = jnp.stack(grads_in)[:, None]
    return (output, input_grad) + tuple(summed)


def solution(mesh):
    return jax.shard_map(
        per_device,
        mesh=mesh,
        in_specs=(
            P(None, "dp", "seq", None),
            P(None, "dp", "seq", None),
            P(None, "dp"),
            P("dp", None),
            P("dp", None),
            P("dp"),
            P("dp"),
            P("dp", None),
            P("dp", None),
            P("dp", None),
            P("dp"),
            P("dp"),
            P("dp", None),
            P("dp", None),
            P("dp"),
            P("dp"),
            P("dp", None),
            P("dp", None),
            P("dp", None),
            P("dp"),
            P("dp"),
        ),
        out_specs=(
            P(None, "dp", "seq", None),
            P(None, "dp", "seq", None),
            P("dp", None),
            P("dp", None),
            P("dp"),
            P("dp"),
            P("dp", None),
            P("dp", None),
            P("dp", None),
            P("dp"),
            P("dp"),
            P("dp", None),
            P("dp", None),
            P("dp"),
            P("dp"),
            P("dp", None),
            P("dp", None),
            P("dp", None),
            P("dp"),
            P("dp"),
        ),
        check_vma=False,
    )
```

profile of v0, /device:TPU:10, one launch (start us, length us, event | category | flops | bytes accessed | tf_op | source)
XLA Modules:
  0.0 2087.9 jit_solution(12031487741407033031)
XLA Ops:
  8.2 32.5 %all-gather.19.cloned.1.call-done = bf16[768,2304]{1,0:T(8,128)(2,1)} async-done(((bf16[192,2304]{1,0:T(8,128)(2,1)}), bf16[768,2304]{1,0:T(8,128)(2,1)}) %all-gather.19.cloned.1.call-update) | async-done | bytes 3538960 | tf_op jit(solution)/shard_map/all_gather | solution.py:270
  67.2 12.9 all-reduce.19
  97.7 40.6 %all-gather.21.cloned.1.call-done = bf16[1024,768]{1,0:T(8,128)(2,1)} async-done(((bf16[128,768]{1,0:T(8,128)(2,1)}), bf16[1024,768]{1,0:T(8,128)(2,1)}) %all-gather.21.cloned.1.call-update) | async-done | bytes 1572880 | tf_op jit(solution)/shard_map/all_gather | solution.py:75
  140.1 4.9 fusion.50
  145.1 9.7 all-gather.25.cloned.1.call-done
  156.9 36.8 %all-gather.27.cloned.1.call-done = bf16[768,3072]{1,0:T(8,128)(2,1)} async-done(((bf16[192,3072]{1,0:T(8,128)(2,1)}), bf16[768,3072]{1,0:T(8,128)(2,1)}) %all-gather.27.cloned.1.call-update) | async-done | bytes 4718608 | tf_op jit(solution)/shard_map/all_gather | solution.py:270
  193.6 4.3 fusion.149
  197.9 34.6 %all-gather.29.cloned.1.call-done = bf16[768,3072]{1,0:T(8,128)(2,1)} async-done(((bf16[192,3072]{1,0:T(8,128)(2,1)}), bf16[768,3072]{1,0:T(8,128)(2,1)}) %all-gather.29.cloned.1.call-update) | async-done | bytes 4718608 | tf_op jit(solution)/shard_map/all_gather | solution.py:270
  232.5 5.0 multiply_convert_fusion.19
  237.6 34.0 %all-gather.31.cloned.1.call-done = bf16[3072,768]{1,0:T(8,128)(2,1)} async-done(((bf16[768,768]{1,0:T(8,128)(2,1)}), bf16[3072,768]{1,0:T(8,128)(2,1)}) %all-gather.31.cloned.1.call-update) | async-done | bytes 4718608 | tf_op jit(solution)/shard_map/all_gather | solution.py:270
  275.1 28.9 %all-gather.33.cloned.1.call-done = bf16[768,2304]{1,0:T(8,128)(2,1)} async-done(((bf16[192,2304]{1,0:T(8,128)(2,1)}), bf16[768,2304]{1,0:T(8,128)(2,1)}) %all-gather.33.cloned.1.call-update) | async-done | bytes 3538960 | tf_op jit(solution)/shard_map/all_gather | solution.py:270
  314.9 37.3 %all-gather.47.cloned.1.call-done = bf16[1024,768]{1,0:T(8,128)(2,1)} async-done(((bf16[128,768]{1,0:T(8,128)(2,1)}), bf16[1024,768]{1,0:T(8,128)(2,1)}) %all-gather.47.cloned.1.call-update) | async-done | bytes 1572880 | tf_op jit(solution)/shard_map/all_gather | solution.py:75
  354.0 43.0 %all-gather.49.cloned.1.call-done = bf16[1024,768]{0,1:T(8,128)(2,1)} async-done(((bf16[128,768]{0,1:T(8,128)(2,1)}), bf16[1024,768]{0,1:T(8,128)(2,1)}) %all-gather.49.cloned.1.call-update) | async-done | bytes 1572880 | tf_op jit(solution)/shard_map/all_gather | solution.py:74
  419.6 24.4 %all-gather.35.cloned.1.call-done = bf16[1024,768]{1,0:T(8,128)(2,1)} async-done(((bf16[128,768]{1,0:T(8,128)(2,1)}), bf16[1024,768]{1,0:T(8,128)(2,1)}) %all-gather.35.cloned.1.call-update) | async-done | bytes 1572880 | tf_op jit(solution)/shard_map/all_gather | solution.py:75
  445.7 43.0 %all-gather.37.cloned.1.call-done = bf16[1024,768]{0,1:T(8,128)(2,1)} async-done(((bf16[128,768]{0,1:T(8,128)(2,1)}), bf16[1024,768]{0,1:T(8,128)(2,1)}) %all-gather.37.cloned.1.call-update) | async-done | bytes 1572880 | tf_op jit(solution)/shard_map/all_gather | solution.py:74
  495.8 10.7 all-gather.39.cloned.1.call-done
  508.2 46.4 %all-gather.51.cloned.1.call-done = bf16[1024,768]{1,0:T(8,128)(2,1)} async-done(((bf16[128,768]{1,0:T(8,128)(2,1)}), bf16[1024,768]{1,0:T(8,128)(2,1)}) %all-gather.51.cloned.1.call-update) | async-done | bytes 1572880 | tf_op jit(solution)/shard_map/all_gather | solution.py:75
  557.2 42.2 %all-gather.53.cloned.1.call-done = bf16[1024,768]{0,1:T(8,128)(2,1)} async-done(((bf16[128,768]{0,1:T(8,128)(2,1)}), bf16[1024,768]{0,1:T(8,128)(2,1)}) %all-gather.53.cloned.1.call-update) | async-done | bytes 1572880 | tf_op jit(solution)/shard_map/all_gather | solution.py:74
  609.4 27.7 %all-gather.41.cloned.1.call-done = bf16[768,3072]{1,0:T(8,128)(2,1)} async-done(((bf16[192,3072]{1,0:T(8,128)(2,1)}), bf16[768,3072]{1,0:T(8,128)(2,1)}) %all-gather.41.cloned.1.call-update) | async-done | bytes 4718608 | tf_op jit(solution)/shard_map/all_gather | solution.py:270
  637.0 4.3 fusion.152
  641.3 34.6 %all-gather.43.cloned.1.call-done = bf16[768,3072]{1,0:T(8,128)(2,1)} async-done(((bf16[192,3072]{1,0:T(8,128)(2,1)}), bf16[768,3072]{1,0:T(8,128)(2,1)}) %all-gather.43.cloned.1.call-update) | async-done | bytes 4718608 | tf_op jit(solution)/shard_map/all_gather | solution.py:270
  675.9 5.0 multiply_convert_fusion.16
  680.9 33.9 %all-gather.45.cloned.1.call-done = bf16[3072,768]{1,0:T(8,128)(2,1)} async-done(((bf16[768,768]{1,0:T(8,128)(2,1)}), bf16[3072,768]{1,0:T(8,128)(2,1)}) %all-gather.45.cloned.1.call-update) | async-done | bytes 4718608 | tf_op jit(solution)/shard_map/all_gather | solution.py:270
  739.8 5.5 multiply_reduce_fusion.3
  750.7 4.2 fusion.29
  761.0 4.6 multiply_reduce_fusion.1
  773.1 5.4 fusion.35
  781.4 4.4 fusion.44
  785.9 30.3 %reduce-scatter.55.cloned.1.call-done = bf16[128,768]{1,0:T(8,128)(2,1)} async-done(((bf16[1024,768]{1,0:T(8,128)(2,1)}), bf16[128,768]{1,0:T(8,128)(2,1)}) %reduce-scatter.55.cloned.1.call-update) | async-done | bytes 196624
  821.4 62.7 %reduce-scatter.57.cloned.1.call-done = bf16[128,768]{1,0:T(8,128)(2,1)} async-done(((bf16[1024,768]{1,0:T(8,128)(2,1)}), bf16[128,768]{1,0:T(8,128)(2,1)}) %reduce-scatter.57.cloned.1.call-update) | async-done | bytes 196624
  885.9 4.5 multiply_reduce_fusion.11
  890.7 5.2 multiply_convert_fusion.12
  904.2 5.7 multiply_reduce_fusion.2
  922.4 28.9 %reduce-scatter.63.cloned.1.call-done = bf16[128,768]{1,0:T(8,128)(2,1)} async-done(((bf16[1024,768]{1,0:T(8,128)(2,1)}), bf16[128,768]{1,0:T(8,128)(2,1)}) %reduce-scatter.63.cloned.1.call-update) | async-done | bytes 196624
  953.2 5.4 fusion.32
  964.8 54.6 %reduce-scatter.65.cloned.1.call-done = bf16[128,768]{1,0:T(8,128)(2,1)} async-done(((bf16[1024,768]{1,0:T(8,128)(2,1)}), bf16[128,768]{1,0:T(8,128)(2,1)}) %reduce-scatter.65.cloned.1.call-update) | async-done | bytes 196624
  1020.6 66.7 %reduce-scatter.59.cloned.1.call-done = bf16[128,768]{1,0:T(8,128)(2,1)} async-done(((bf16[1024,768]{1,0:T(8,128)(2,1)}), bf16[128,768]{1,0:T(8,128)(2,1)}) %reduce-scatter.59.cloned.1.call-update) | async-done | bytes 196624
  1093.7 4.4 multiply_convert_fusion.8
  1104.1 4.6 multiply_reduce_fusion
  1115.2 5.4 fusion.38
  1123.2 32.1 %reduce-scatter.61.cloned.1.call-done = bf16[128,768]{1,0:T(8,128)(2,1)} async-done(((bf16[1024,768]{1,0:T(8,128)(2,1)}), bf16[128,768]{1,0:T(8,128)(2,1)}) %reduce-scatter.61.cloned.1.call-update) | async-done | bytes 196624
  1162.6 4.0 fusion.63
  1166.6 56.6 %reduce-scatter.67.cloned.1.call-done = bf16[128,768]{1,0:T(8,128)(2,1)} async-done(((bf16[1024,768]{1,0:T(8,128)(2,1)}), bf16[128,768]{1,0:T(8,128)(2,1)}) %reduce-scatter.67.cloned.1.call-update) | async-done | bytes 196624
  1224.5 66.7 %reduce-scatter.69.cloned.1.call-done = bf16[128,768]{1,0:T(8,128)(2,1)} async-done(((bf16[1024,768]{1,0:T(8,128)(2,1)}), bf16[128,768]{1,0:T(8,128)(2,1)}) %reduce-scatter.69.cloned.1.call-update) | async-done | bytes 196624
  1292.2 6.0 fusion.4
  1298.3 5.8 copy.124
  1311.1 3.6 add_convert_fusion
  1317.3 3.6 add_convert_fusion.1
  1323.5 3.5 add_convert_fusion.2
  1335.3 3.7 add_convert_fusion.3
  1341.5 3.6 add_convert_fusion.4
  1347.7 3.6 add_convert_fusion.5
  1353.8 18.4 reduce-scatter.47.cloned.1.call-done
  1372.2 28.9 %reduce-scatter.37.cloned.1.call-done = bf16[192,768]{1,0:T(8,128)(2,1)} async-done(((bf16[768,768]{1,0:T(8,128)(2,1)}), bf16[192,768]{1,0:T(8,128)(2,1)}) %reduce-scatter.37.cloned.1.call-update) | async-done | bytes 294928 | tf_op jit(solution)/shard_map/reduce_scatter | solution.py:285
  1401.1 50.4 %reduce-scatter.53.cloned.1.call-done = bf16[768,768]{1,0:T(8,128)(2,1)} async-done(((bf16[3072,768]{1,0:T(8,128)(2,1)}), bf16[768,768]{1,0:T(8,128)(2,1)}) %reduce-scatter.53.cloned.1.call-update) | async-done | bytes 1179664 | tf_op jit(solution)/shard_map/reduce_scatter | solution.py:285
  1451.5 50.4 %reduce-scatter.51.cloned.1.call-done = bf16[192,3072]{1,0:T(8,128)(2,1)} async-done(((bf16[768,3072]{1,0:T(8,128)(2,1)}), bf16[192,3072]{1,0:T(8,128)(2,1)}) %reduce-scatter.51.cloned.1.call-update) | async-done | bytes 1179664 | tf_op jit(solution)/shard_map/reduce_scatter | solution.py:285
  1501.9 50.6 %reduce-scatter.49.cloned.1.call-done = bf16[192,3072]{1,0:T(8,128)(2,1)} async-done(((bf16[768,3072]{1,0:T(8,128)(2,1)}), bf16[192,3072]{1,0:T(8,128)(2,1)}) %reduce-scatter.49.cloned.1.call-update) | async-done | bytes 1179664 | tf_op jit(solution)/shard_map/reduce_scatter | solution.py:285
  1552.5 42.8 %reduce-scatter.45.cloned.1.call-done = bf16[192,2304]{1,0:T(8,128)(2,1)} async-done(((bf16[768,2304]{1,0:T(8,128)(2,1)}), bf16[192,2304]{1,0:T(8,128)(2,1)}) %reduce-scatter.45.cloned.1.call-update) | async-done | bytes 884752 | tf_op jit(solution)/shard_map/reduce_scatter | solution.py:285
  1595.4 50.6 %reduce-scatter.43.cloned.1.call-done = bf16[768,768]{1,0:T(8,128)(2,1)} async-done(((bf16[3072,768]{1,0:T(8,128)(2,1)}), bf16[768,768]{1,0:T(8,128)(2,1)}) %reduce-scatter.43.cloned.1.call-update) | async-done | bytes 1179664 | tf_op jit(solution)/shard_map/reduce_scatter | solution.py:285
  1645.9 50.4 %reduce-scatter.41.cloned.1.call-done = bf16[192,3072]{1,0:T(8,128)(2,1)} async-done(((bf16[768,3072]{1,0:T(8,128)(2,1)}), bf16[192,3072]{1,0:T(8,128)(2,1)}) %reduce-scatter.41.cloned.1.call-update) | async-done | bytes 1179664 | tf_op jit(solution)/shard_map/reduce_scatter | solution.py:285
  1696.4 50.4 %reduce-scatter.39.cloned.1.call-done = bf16[192,3072]{1,0:T(8,128)(2,1)} async-done(((bf16[768,3072]{1,0:T(8,128)(2,1)}), bf16[192,3072]{1,0:T(8,128)(2,1)}) %reduce-scatter.39.cloned.1.call-update) | async-done | bytes 1179664 | tf_op jit(solution)/shard_map/reduce_scatter | solution.py:285
  1757.7 13.2 all-reduce.18
  1779.4 20.2 all-reduce.16
  1817.0 248.4 %all-reduce.22.cloned.1.call-done = (bf16[192,2304]{0,1:T(8,128)(2,1)}, bf16[192,768]{1,0:T(8,128)(2,1)}, bf16[192,3072]{1,0:T(8,128)(2,1)}, bf16[192,3072]{1,0:...) async-done(((bf16[192,2304]{0,1:T(8,128)(2,1)}, ...) | async-done | bytes 9437200 | tf_op jit(solution)/shard_map/psum | solution.py:288
  (902 shorter events, 300.0 us)
Async XLA Ops:
  7.2 33.4 %all-gather.19.cloned.1.call-start = ((), (), s32[]{:S(2)}) async-start(), calls=%async_computation.18 | async-start | bytes 4423680 | tf_op jit(solution)/shard_map/all_gather | solution.py:270
  7.9 83.4 %all-gather.23.cloned.1.call-start = ((), (), s32[]{:S(2)}) async-start(), calls=%async_computation.20 | async-start | bytes 1769472 | tf_op jit(solution)/shard_map/all_gather | solution.py:74
  46.3 92.0 %all-gather.21.cloned.1.call-start = ((), (), s32[]{:S(2)}) async-start(), calls=%async_computation.19 | async-start | bytes 1769472 | tf_op jit(solution)/shard_map/all_gather | solution.py:75
  48.4 106.3 %all-gather.25.cloned.1.call-start = ((), (), s32[]{:S(2)}) async-start(), calls=%async_computation.21 | async-start | bytes 1474560 | tf_op jit(solution)/shard_map/all_gather | solution.py:270
  49.0 144.6 %all-gather.27.cloned.1.call-start = ((), (), s32[]{:S(2)}) async-start(), calls=%async_computation.22 | async-start | bytes 5898240 | tf_op jit(solution)/shard_map/all_gather | solution.py:270
  49.6 182.9 %all-gather.29.cloned.1.call-start = ((), (), s32[]{:S(2)}) async-start(), calls=%async_computation.23 | async-start | bytes 5898240 | tf_op jit(solution)/shard_map/all_gather | solution.py:270
  50.2 221.4 %all-gather.31.cloned.1.call-start = ((), (), s32[]{:S(2)}) async-start(), calls=%async_computation.24 | async-start | bytes 5898240 | tf_op jit(solution)/shard_map/all_gather | solution.py:270
  50.9 253.0 %all-gather.33.cloned.1.call-start = ((), (), s32[]{:S(2)}) async-start(), calls=%async_computation.25 | async-start | bytes 4423680 | tf_op jit(solution)/shard_map/all_gather | solution.py:270
  51.7 300.6 %all-gather.47.cloned.1.call-start = ((), (), s32[]{:S(2)}) async-start(), calls=%async_computation.32 | async-start | bytes 1769472 | tf_op jit(solution)/shard_map/all_gather | solution.py:75
  90.1 306.9 %all-gather.49.cloned.1.call-start = ((), (), s32[]{:S(2)}) async-start(), calls=%async_computation.33 | async-start | bytes 1769472 | tf_op jit(solution)/shard_map/all_gather | solution.py:74
  156.4 115.1 %copy-start.19 = (f32[128,768]{1,0:T(8,128)}, f32[128,768]{1,0:T(8,128)S(1)}, u32[]{:S(2)}) copy-start(f32[128,768]{1,0:T(8,128)S(1)} %get-tuple-element.244) | copy-start | bytes 1179652
  156.5 115.1 %copy-start.201 = (f32[128]{0:T(128)}, f32[128]{0:T(128)S(1)}, u32[]{:S(2)}) copy-start(f32[128]{0:T(128)S(1)} %broadcast_multiply_fusion.7) | copy-start | bytes 1540
  156.7 114.9 %copy-start.211 = (f32[128]{0:T(128)}, f32[128]{0:T(128)S(1)}, u32[]{:S(2)}) copy-start(f32[128]{0:T(128)S(1)} %fusion.81) | copy-start | bytes 1540
  156.9 75.7 %copy-start.74 = (bf16[128,768]{1,0:T(8,128)(2,1)}, bf16[128,768]{1,0:T(8,128)(2,1)S(1)}, u32[]{:S(2)}) copy-start(bf16[128,768]{1,0:T(8,128)(2,1)S(1)} %fusion.57) | copy-start | bytes 589828
  310.5 86.5 %copy-start.104 = (bf16[128,12,32]{0,2,1:T(8,128)(2,1)S(1)}, bf16[128,12,32]{0,2,1:T(8,128)(2,1)}, u32[]{:S(2)}) copy-start(bf16[128,12,32]{0,2,1:T(8,128)(2,1)} %get-tuple-element.218) | copy-start | bytes 294916
  310.5 86.5 %copy-start.106 = (bf16[128,12,32]{0,2,1:T(8,128)(2,1)S(1)}, bf16[128,12,32]{0,2,1:T(8,128)(2,1)}, u32[]{:S(2)}) copy-start(bf16[128,12,32]{0,2,1:T(8,128)(2,1)} %get-tuple-element.219) | copy-start | bytes 294916
  311.2 132.7 %all-gather.35.cloned.1.call-start = ((), (), s32[]{:S(2)}) async-start(), calls=%async_computation.26 | async-start | bytes 1769472 | tf_op jit(solution)/shard_map/all_gather | solution.py:75
  312.4 176.2 %all-gather.37.cloned.1.call-start = ((), (), s32[]{:S(2)}) async-start(), calls=%async_computation.27 | async-start | bytes 1769472 | tf_op jit(solution)/shard_map/all_gather | solution.py:74
  314.1 192.3 %all-gather.39.cloned.1.call-start = ((), (), s32[]{:S(2)}) async-start(), calls=%async_computation.28 | async-start | bytes 1474560 | tf_op jit(solution)/shard_map/all_gather | solution.py:270
  314.9 239.7 %all-gather.51.cloned.1.call-start = ((), (), s32[]{:S(2)}) async-start(), calls=%async_computation.34 | async-start | bytes 1769472 | tf_op jit(solution)/shard_map/all_gather | solution.py:75
  410.2 196.4 %copy-start.21 = (f32[128,768]{1,0:T(8,128)}, f32[128,768]{1,0:T(8,128)S(1)}, u32[]{:S(2)}) copy-start(f32[128,768]{1,0:T(8,128)S(1)} %get-tuple-element.260) | copy-start | bytes 1179652
  413.1 186.2 %all-gather.53.cloned.1.call-start = ((), (), s32[]{:S(2)}) async-start(), calls=%async_computation.35 | async-start | bytes 1769472 | tf_op jit(solution)/shard_map/all_gather | solution.py:74
  414.4 184.9 %copy-start.116 = (bf16[128,12,32]{0,2,1:T(8,128)(2,1)}, bf16[128,12,32]{0,2,1:T(8,128)(2,1)S(1)}, u32[]{:S(2)}) copy-start(bf16[128,12,32]{0,2,1:T(8,128)(2,1)S(1)} %get-tuple-element.196) | copy-start | bytes 294916
  414.4 184.9 %copy-start.118 = (bf16[128,12,32]{0,2,1:T(8,128)(2,1)}, bf16[128,12,32]{0,2,1:T(8,128)(2,1)S(1)}, u32[]{:S(2)}) copy-start(bf16[128,12,32]{0,2,1:T(8,128)(2,1)S(1)} %get-tuple-element.197) | copy-start | bytes 294916
  415.2 73.5 %copy-start.108 = (bf16[128,12,32]{0,2,1:T(8,128)(2,1)S(1)}, bf16[128,12,32]{0,2,1:T(8,128)(2,1)}, u32[]{:S(2)}) copy-start(bf16[128,12,32]{0,2,1:T(8,128)(2,1)} %get-tuple-element.188) | copy-start | bytes 294916
  415.2 73.5 %copy-start.110 = (bf16[128,12,32]{0,2,1:T(8,128)(2,1)S(1)}, bf16[128,12,32]{0,2,1:T(8,128)(2,1)}, u32[]{:S(2)}) copy-start(bf16[128,12,32]{0,2,1:T(8,128)(2,1)} %get-tuple-element.189) | copy-start | bytes 294916
  415.2 221.8 %all-gather.41.cloned.1.call-start = ((), (), s32[]{:S(2)}) async-start(), calls=%async_computation.29 | async-start | bytes 5898240 | tf_op jit(solution)/shard_map/all_gather | solution.py:270
  415.8 260.1 %all-gather.43.cloned.1.call-start = ((), (), s32[]{:S(2)}) async-start(), calls=%async_computation.30 | async-start | bytes 5898240 | tf_op jit(solution)/shard_map/all_gather | solution.py:270
  416.4 298.4 %all-gather.45.cloned.1.call-start = ((), (), s32[]{:S(2)}) async-start(), calls=%async_computation.31 | async-start | bytes 5898240 | tf_op jit(solution)/shard_map/all_gather | solution.py:270
  417.0 399.2 %reduce-scatter.55.cloned.1.call-start = ((), (), s32[]{:S(2)}) async-start(), calls=%async_computation.45 | async-start | bytes 1769472
  418.9 189.6 %copy-start.165 = (f32[768]{0:T(1024)}, f32[768]{0:T(1024)S(1)}, u32[]{:S(2)}) copy-start(f32[768]{0:T(1024)S(1)} %convert_element_type.535) | copy-start | bytes 9220
  419.0 189.5 %copy-start.179 = (f32[768]{0:T(1024)}, f32[768]{0:T(1024)S(1)}, u32[]{:S(2)}) copy-start(f32[768]{0:T(1024)S(1)} %convert_element_type.536) | copy-start | bytes 9220
  495.8 106.1 %copy-start.129 = (bf16[12,64,128]{2,1,0:T(8,128)(2,1)}, bf16[12,64,128]{2,1,0:T(8,128)(2,1)S(1)}, u32[]{:S(2)}) copy-start(bf16[12,64,128]{2,1,0:T(8,128)(2,1)S(1)} %fusion.49) | copy-start | bytes 589828
  609.4 66.6 %copy-start.84 = (bf16[128,768]{1,0:T(8,128)(2,1)}, bf16[128,768]{1,0:T(8,128)(2,1)S(1)}, u32[]{:S(2)}) copy-start(bf16[128,768]{1,0:T(8,128)(2,1)S(1)} %get-tuple-element.229) | copy-start | bytes 589828
  750.7 133.4 %reduce-scatter.57.cloned.1.call-start = ((), (), s32[]{:S(2)}) async-start(), calls=%async_computation.46 | async-start | bytes 1769472
  756.6 194.7 %reduce-scatter.63.cloned.1.call-start = ((), (), s32[]{:S(2)}) async-start(), calls=%async_computation.49 | async-start | bytes 1769472
  771.7 247.8 %reduce-scatter.65.cloned.1.call-start = ((), (), s32[]{:S(2)}) async-start(), calls=%async_computation.50 | async-start | bytes 1769472
  785.8 301.4 %reduce-scatter.59.cloned.1.call-start = ((), (), s32[]{:S(2)}) async-start(), calls=%async_computation.47 | async-start | bytes 1769472
  917.5 237.8 %reduce-scatter.61.cloned.1.call-start = ((), (), s32[]{:S(2)}) async-start(), calls=%async_computation.48 | async-start | bytes 1769472
  964.7 123.7 %copy-start.91 = (f32[128,12,64]{0,2,1:T(8,128)S(1)}, f32[128,12,64]{0,2,1:T(8,128)}, u32[]{:S(2)}) copy-start(f32[128,12,64]{0,2,1:T(8,128)} %fusion.42) | copy-start | bytes 1179652
  964.7 123.7 %copy-start.92 = (f32[128,12,64]{0,2,1:T(8,128)S(1)}, f32[128,12,64]{0,2,1:T(8,128)}, u32[]{:S(2)}) copy-start(f32[128,12,64]{0,2,1:T(8,128)} %fusion.43) | copy-start | bytes 1179652
  964.7 123.7 %copy-start.93 = (f32[128,12,64]{0,2,1:T(8,128)S(1)}, f32[128,12,64]{0,2,1:T(8,128)}, u32[]{:S(2)}) copy-start(f32[128,12,64]{0,2,1:T(8,128)} %convert.170) | copy-start | bytes 1179652
  964.7 125.6 %copy-start.22 = (f32[128,768]{1,0:T(8,128)S(1)}, f32[128,768]{1,0:T(8,128)}, u32[]{:S(2)}) copy-start(f32[128,768]{1,0:T(8,128)} %copy-done.21) | copy-start | bytes 1179652
  964.7 125.6 %copy-start.47 = (f32[128,768]{1,0:T(8,128)S(1)}, f32[128,768]{1,0:T(8,128)}, u32[]{:S(2)}) copy-start(f32[128,768]{1,0:T(8,128)} %copy-done.46) | copy-start | bytes 1179652
  964.8 258.4 %reduce-scatter.67.cloned.1.call-start = ((), (), s32[]{:S(2)}) async-start(), calls=%async_computation.51 | async-start | bytes 1769472
  1020.5 72.8 %copy-start.143 = (bf16[128,768]{0,1:T(8,128)(2,1)}, bf16[128,768]{0,1:T(8,128)(2,1)S(1)}, u32[]{:S(2)}) copy-start(bf16[128,768]{0,1:T(8,128)(2,1)S(1)} %copy.119) | copy-start | bytes 589828
  1114.9 176.2 %reduce-scatter.69.cloned.1.call-start = ((), (), s32[]{:S(2)}) async-start(), calls=%async_computation.52 | async-start | bytes 1769472
  1123.2 228.2 %reduce-scatter.71.cloned.1.call-start = ((), (), s32[]{:S(2)}) async-start(), calls=%async_computation.53 | async-start | bytes 4423680
  1162.5 61.7 %copy-start.94 = (f32[128,12,64]{0,2,1:T(8,128)S(1)}, f32[128,12,64]{0,2,1:T(8,128)}, u32[]{:S(2)}) copy-start(f32[128,12,64]{0,2,1:T(8,128)} %fusion.41) | copy-start | bytes 1179652
  1166.6 125.7 %copy-start.44 = (bf16[2,1,128,768]{3,2,1,0:T(8,128)(2,1)S(1)}, bf16[2,1,128,768]{3,2,1,0:T(8,128)(2,1)}, u32[]{:S(2)}) copy-start(bf16[2,1,128,768]{3,2,1,0:T(8,128)(2,1)} %param.21) | copy-start | bytes 1179652
  1224.4 73.8 %copy-start.134 = (bf16[128,12,64]{0,2,1:T(8,128)(2,1)}, bf16[128,12,64]{0,2,1:T(8,128)(2,1)S(1)}, u32[]{:S(2)}) copy-start(bf16[128,12,64]{0,2,1:T(8,128)(2,1)S(1)} %pad_maximum_fusion.26) | copy-start | bytes 589828
  1224.4 73.8 %copy-start.137 = (bf16[128,12,64]{0,2,1:T(8,128)(2,1)}, bf16[128,12,64]{0,2,1:T(8,128)(2,1)S(1)}, u32[]{:S(2)}) copy-start(bf16[128,12,64]{0,2,1:T(8,128)(2,1)S(1)} %pad_maximum_fusion.27) | copy-start | bytes 589828
  1304.1 68.1 %reduce-scatter.47.cloned.1.call-start = ((), (), s32[]{:S(2)}) async-start(), calls=%async_computation.41 | async-start | bytes 1474560 | tf_op jit(solution)/shard_map/reduce_scatter | solution.py:285
  1307.3 93.8 %reduce-scatter.37.cloned.1.call-start = ((), (), s32[]{:S(2)}) async-start(), calls=%async_computation.36 | async-start | bytes 1474560 | tf_op jit(solution)/shard_map/reduce_scatter | solution.py:285
  1309.6 142.0 %reduce-scatter.53.cloned.1.call-start = ((), (), s32[]{:S(2)}) async-start(), calls=%async_computation.44 | async-start | bytes 5898240 | tf_op jit(solution)/shard_map/reduce_scatter | solution.py:285
  1314.8 187.1 %reduce-scatter.51.cloned.1.call-start = ((), (), s32[]{:S(2)}) async-start(), calls=%async_computation.43 | async-start | bytes 5898240 | tf_op jit(solution)/shard_map/reduce_scatter | solution.py:285
  1321.0 231.6 %reduce-scatter.49.cloned.1.call-start = ((), (), s32[]{:S(2)}) async-start(), calls=%async_computation.42 | async-start | bytes 5898240 | tf_op jit(solution)/shard_map/reduce_scatter | solution.py:285
  1327.2 268.2 %reduce-scatter.45.cloned.1.call-start = ((), (), s32[]{:S(2)}) async-start(), calls=%async_computation.40 | async-start | bytes 4423680 | tf_op jit(solution)/shard_map/reduce_scatter | solution.py:285
  1332.6 313.3 %reduce-scatter.43.cloned.1.call-start = ((), (), s32[]{:S(2)}) async-start(), calls=%async_computation.39 | async-start | bytes 5898240 | tf_op jit(solution)/shard_map/reduce_scatter | solution.py:285
  1339.0 357.4 %reduce-scatter.41.cloned.1.call-start = ((), (), s32[]{:S(2)}) async-start(), calls=%async_computation.38 | async-start | bytes 5898240 | tf_op jit(solution)/shard_map/reduce_scatter | solution.py:285
  1345.2 401.6 %reduce-scatter.39.cloned.1.call-start = ((), (), s32[]{:S(2)}) async-start(), calls=%async_computation.37 | async-start | bytes 5898240 | tf_op jit(solution)/shard_map/reduce_scatter | solution.py:285
  1351.4 714.0 %all-reduce.22.cloned.1.call-start = ((), (), s32[]{:S(2)}) async-start(), calls=%async_computation.54 | async-start | bytes 19464192 | tf_op jit(solution)/shard_map/psum | solution.py:288
  1746.8 63.3 %copy-start.178 = (f32[768]{0:T(1024)S(1)}, f32[768]{0:T(1024)}, u32[]{:S(2)}) copy-start(f32[768]{0:T(1024)} %convert_element_type.539) | copy-start | bytes 9220
  1746.8 65.5 %copy-start.14 = (bf16[768,2304]{1,0:T(8,128)(2,1)S(1)}, bf16[768,2304]{1,0:T(8,128)(2,1)}, u32[]{:S(2)}) copy-start(bf16[768,2304]{1,0:T(8,128)(2,1)} %all-gather.19.cloned.1.call-done) | copy-start | bytes 10616836
  (255 other events, 1637.5 us)
Sparse Core Ops, SparseCore 0:
  9.6 30.9 all-gather.18
  46.4 44.8 all-gather.22
  94.0 44.2 all-gather.20
  139.7 14.9 all-gather.24
  156.1 37.4 all-gather.26
  195.0 37.4 all-gather.28
  234.1 37.4 all-gather.30
  273.1 30.7 all-gather.32
  306.7 45.4 all-gather.46
  354.7 42.2 all-gather.48
  399.7 44.1 all-gather.34
  446.4 42.2 all-gather.36
  490.2 16.1 all-gather.38
  509.1 45.4 all-gather.50
  557.1 42.2 all-gather.52
  600.8 36.1 all-gather.40
  638.4 37.4 all-gather.42
  677.3 37.4 all-gather.44
  750.8 65.3 reduce-scatter.54
  820.4 63.6 reduce-scatter.56
  887.6 63.7 reduce-scatter.62
  955.7 63.7 reduce-scatter.64
  1023.5 63.7 reduce-scatter.58
  1091.5 63.7 reduce-scatter.60
  1159.3 63.7 reduce-scatter.66
  1227.4 63.7 reduce-scatter.68
  1304.2 38.8 reduce-scatter.70
  1346.4 25.7 reduce-scatter.46
  1375.3 25.7 reduce-scatter.36
  1403.6 47.8 reduce-scatter.52
  1454.1 47.8 reduce-scatter.50
  1504.6 47.8 reduce-scatter.48
  1554.9 40.3 reduce-scatter.44
  1598.1 47.8 reduce-scatter.42
  1648.5 47.8 reduce-scatter.40
  1698.9 47.8 reduce-scatter.38
  1753.4 311.9 all-reduce.21
where the time goes:
time: 2100 us; the launch traced here: 2090 us
  waiting for transfers between devices  1610 us (77%)
  matrix products  219 us (10%)
  local copies, waits for them, and re-layouts  113 us (5%)
  other arithmetic  78.2 us (4%)
  blocking collectives  46.3 us (2%)
  between operations  21.3 us (1%)
    unnamed x46, waiting for transfers between devices  405 us
    reduce_scatter x9, waiting for transfers between devices, per_device(): lax.psum_scatter(as_sent(totals[index]), 'dp', scatter_dimension=0, tiled...  393 us
    all_gather x10, waiting for transfers between devices, per_device(): full = lax.all_gather(as_sent(local_sets[index]), 'dp', axis=0, tiled=True)  283 us
    psum x1, waiting for transfers between devices, per_device(): lax.psum(as_sent(shares), 'seq')  248 us
    all_gather x4, waiting for transfers between devices, forward_layer(): lax.all_gather(values_r, 'seq', axis=0, tiled=True)  149 us
    all_gather x4, waiting for transfers between devices, forward_layer(): lax.all_gather(keys_r, 'seq', axis=0, tiled=True)  129 us
    unnamed x608, local copies, waits for them, and re-layouts  92.8 us
    dot_general x20, matrix products, dot_first(): lax.dot_general(left, right, (((0,), (0,)), ((), ())), preferred_element_...  48.6 us
  transfers between devices with their start and end apart: 37, of which 36 were waited for; matrix products, arithmetic and copies ran while one was open for 15% of the time, Pallas kernels for 0%

commit v1 on v0

--- a/solution.py
+++ b/solution.py
@@ -1,9 +1,783 @@
+import functools
+
 import jax
 import jax.numpy as jnp
 from jax import lax
+from jax.experimental import pallas as pl
+from jax.experimental.pallas import tpu as pltpu
 from jax.sharding import PartitionSpec as P
 
 HEAD = 64
+
+DP = 4
+SQ = 8
+TOK = 128
+PART = TOK // DP
+ROWS = TOK + PART
+ALL = DP * ROWS
+HALF = 2 * ROWS
+D = 768
+LEN = SQ * TOK
+QB = 256
+F32 = jnp.float32
+BF16 = jnp.bfloat16
+MESH = pl.DeviceIdType.MESH
+
+
+def mm(a, b):
+    return lax.dot_general(a, b, (((1,), (0,)), ((), ())), preferred_element_type=F32)
+
+
+def mm_t(a, b):
+    return lax.dot_general(a, b, (((1,), (1,)), ((), ())), preferred_element_type=F32)
+
+
+def t_mm(a, b):
+    return lax.dot_general(a, b, (((0,), (0,)), ((), ())), preferred_element_type=F32)
+
+
+def low_lanes(shape):
+    return lax.rem(lax.broadcasted_iota(jnp.int32, shape, len(shape) - 1), 128) < 64
+
+
+def swap_halves(x):
+    lane = lax.broadcasted_iota(jnp.int32, x.shape, 1)
+    return jnp.where(lax.rem(lane, 64) < 32, pltpu.roll(x, 96, 1), pltpu.roll(x, 32, 1))
+
+
+class Links:
+    def __init__(self, send, recv):
+        self.send, self.recv, self.used, self.sent = send, recv, 0, []
+        self.d = lax.axis_index("dp")
+        self.s = lax.axis_index("seq")
+        self.x = self.d // 2
+        self.core = lax.rem(self.d, 2)
+        self.sib = 2 * self.x + (1 - self.core)
+        self.xp = lax.rem(self.d + 2, DP)
+        self.diag = lax.rem(self.sib + 2, DP)
+        self.z = self.s // 2
+        self.y = lax.rem(self.s, 2)
+        self.dp_peers = [self.xp, self.diag, self.sib]
+        self.seq_peers = [lax.rem(self.s + k, SQ) for k in range(1, SQ)]
+
+    def enter(self, peers):
+        bar = pltpu.get_barrier_semaphore()
+        for p in peers:
+            pl.semaphore_signal(bar, inc=1, device_id=p, device_id_type=MESH)
+        pl.semaphore_wait(bar, len(peers))
+
+    def all_peers(self):
+        return [(p, self.s) for p in self.dp_peers] + [(self.d, p) for p in self.seq_peers]
+
+    def copy(self, src, dst, to):
+        i = self.used
+        self.used += 1
+        c = pltpu.make_async_remote_copy(
+            src_ref=src,
+            dst_ref=dst,
+            send_sem=self.send.at[i],
+            recv_sem=self.recv.at[i],
+            device_id=to,
+            device_id_type=MESH,
+        )
+        c.start()
+        self.sent.append(c)
+        return c
+
+    def drain(self):
+        for c in self.sent:
+            c.wait_send()
+
+
+def block(ref, i, rows=ROWS):
+    return ref.at[pl.ds(pl.multiple_of(i * rows, 16), rows)]
+
+
+def gather_begin(L, ref, rows=ROWS):
+    own = block(ref, L.d, rows)
+    far = L.copy(own, own, (L.xp, L.s))
+    near = L.copy(own, own, (L.sib, L.s))
+    return near, far
+
+
+def gather_forward(L, ref, far, rows=ROWS):
+    far.wait_recv()
+    got = block(ref, L.xp, rows)
+    return L.copy(got, got, (L.sib, L.s))
+
+
+def reduce_own(L, part, bufs):
+    snd, got, mid, fin = bufs
+    snd[0] = block(part, L.sib)[...].astype(BF16)
+    return L.copy(snd.at[0], got.at[0], (L.sib, L.s))
+
+
+def reduce_other(L, part, bufs):
+    snd, got, mid, fin = bufs
+    snd[1] = block(part, L.diag)[...].astype(BF16)
+    return L.copy(snd.at[1], got.at[1], (L.sib, L.s))
+
+
+def reduce_cross(L, part, bufs, c_other):
+    snd, got, mid, fin = bufs
+    c_other.wait_recv()
+    mid[...] = (block(part, L.xp)[...] + got[1].astype(F32)).astype(BF16)
+    return L.copy(mid, fin, (L.xp, L.s))
+
+
+def reduce_end(L, part, bufs, c_own, c_cross):
+    snd, got, mid, fin = bufs
+    c_own.wait_recv()
+    c_cross.wait_recv()
+    return block(part, L.d)[...] + got[0].astype(F32) + fin[...].astype(F32)
+
+
+REDUCE_BUFS = [
+    pltpu.VMEM((2, ROWS, D), BF16),
+    pltpu.VMEM((2, ROWS, D), BF16),
+    pltpu.VMEM((ROWS, D), BF16),
+    pltpu.VMEM((ROWS, D), BF16),
+]
+
+
+def chip_rows(c):
+    return pl.ds(pl.multiple_of(c * HALF, 32), HALF)
+
+
+def token_rows(s):
+    return pl.ds(pl.multiple_of(s * TOK, TOK), TOK)
+
+
+def normalize(res):
+    cen = res - jnp.mean(res, axis=-1, keepdims=True)
+    rstd = lax.rsqrt(jnp.mean(cen * cen, axis=-1, keepdims=True) + 1e-05)
+    return cen * rstd, rstd
+
+
+def normalize_back(grad, gain, xhat, rstd):
+    dn = grad * gain
+    return (dn - jnp.mean(dn, axis=-1, keepdims=True) - xhat * jnp.mean(dn * xhat, axis=-1, keepdims=True)) * rstd
+
+
+def pack_pairs(src, dst):
+    half = dst.shape[-1]
+    one, two = pl.ds(0, half), pl.ds(half, half)
+    keep = low_lanes((TOK, half))
+    for e in range(DP):
+        dst[e] = src[pl.ds(ROWS * e, TOK), one]
+        dst[4, pl.ds(PART * e, PART)] = src[pl.ds(ROWS * e + TOK, PART), one]
+        dst[7, pl.ds(PART * e, PART)] = src[pl.ds(ROWS * e + TOK, PART), two]
+    for p in range(2):
+        a = src[pl.ds(ROWS * 2 * p, TOK), two].astype(F32)
+        b = src[pl.ds(ROWS * (2 * p + 1), TOK), two].astype(F32)
+        dst[5 + p] = jnp.where(keep, a, b).astype(BF16)
+
+
+def unpack_pairs(src, dst):
+    half = src.shape[-1]
+    one, two = pl.ds(0, half), pl.ds(half, half)
+    keep = low_lanes((TOK, half))
+    third = [src[5].astype(F32), src[6].astype(F32)]
+    last = jnp.where(keep, src[7].astype(F32), 0.0).astype(BF16)
+    for e in range(DP):
+        dst[pl.ds(ROWS * e, TOK), one] = src[e]
+        mine = third[e // 2]
+        mine = jnp.where(keep, mine, 0.0) if e % 2 == 0 else jnp.where(keep, 0.0, mine)
+        dst[pl.ds(ROWS * e, TOK), two] = mine.astype(BF16)
+        dst[pl.ds(ROWS * e + TOK, PART), one] = src[4, pl.ds(PART * e, PART)]
+        dst[pl.ds(ROWS * e + TOK, PART), two] = last[PART * e : PART * (e + 1)]
+
+
+def forward_kernel(first, layer, *refs):
+    if first:
+        (inp, livet, cot, nvp, wqs, wg, wu, wo, wd, cosr, sinr) = refs[:11]
+        (o_h, o_x, o_qkv, o_lse, o_ctx, o_ce, o_actf, o_gp, o_up, o_hid, o_xa, o_xf, o_ra, o_rf, o_wq, o_wg, o_wu, o_wo, o_cot, o_lv, o_nv) = refs[11:32]
+        rest = refs[32:]
+        (inb, cbuf, nbuf) = rest[:3]
+        rest = rest[3:]
+        nv = o_nv
+    else:
+        (hin, nv, wqs, wg, wu, wo, wd, cosr, sinr) = refs[:9]
+        (o_h, o_x, o_qkv, o_lse, o_ctx, o_ce, o_actf, o_gp, o_up, o_hid, o_xa, o_xf, o_ra, o_rf, o_wq, o_wg, o_wu, o_wo) = refs[9:27]
+        rest = refs[27:]
+    (part, qx, sbq, cbk, crx, kz) = rest[:6]
+    red_a, red_f = rest[6:10], rest[10:14]
+    send, recv, lsem = rest[14:17]
+    L = Links(send, recv)
+    L.enter(L.all_peers())
+    d, s = L.d, L.s
+    depth = D // DP
+
+    if first:
+        inb[pl.ds(pl.multiple_of(d * 256, 256), 256)] = inp[...].reshape(256, D)
+        o_lv[d] = livet[...]
+        nbuf[d] = nvp[...]
+        small = []
+        for p in L.dp_peers:
+            small.append(L.copy(livet, o_lv.at[d], (p, s)))
+            small.append(L.copy(nvp, nbuf.at[d], (p, s)))
+        near, far = gather_begin(L, inb, 256)
+    else:
+        block(o_x, d)[...] = hin[...].astype(BF16)
+        near, far = gather_begin(L, o_x)
+
+    own = pl.ds(pl.multiple_of(d * depth, 64), depth)
+    qw = [L.copy(wqs.at[p], o_wq.at[own], (p, s)) for p in L.dp_peers]
+    o_wq[own] = wqs[d]
+    cols = [pl.ds(pl.multiple_of(p * D, D), D) for p in L.dp_peers]
+    mine = pl.ds(pl.multiple_of(d * D, D), D)
+    loc = [
+        pltpu.make_async_copy(wg.at[:, mine], o_wg.at[own], lsem.at[0]),
+        pltpu.make_async_copy(wu.at[:, mine], o_wu.at[own], lsem.at[1]),
+    ]
+    for c in loc:
+        c.start()
+    o_wo[pl.ds(0, depth)] = wo[...]
+    o_wo[pl.ds(depth, 64)] = wo[pl.ds(128, 64)]
+
+    def project(rows):
+        y = mm(o_x[rows], o_wq[...])
+        co, si = cosr[rows], sinr[rows]
+        for t in range(6):
+            v = y[:, 128 * t : 128 * (t + 1)]
+            if t % 3 != 2:
+                v = v * co + swap_halves(v) * si
+            if t % 3 == 0:
+                v = v * (HEAD**-0.5)
+            qx[rows, pl.ds(128 * t, 128)] = v.astype(BF16)
+
+    fwd = gather_forward(L, inb if first else o_x, far, 256 if first else ROWS)
+    near.wait_recv()
+    if first:
+        for c in small:
+            c.wait_recv()
+        o_nv[...] = nbuf[0] + nbuf[1] + nbuf[2] + nbuf[3]
+        f0 = o_lv[0, 0:1] * o_lv[1, 0:1] * o_lv[2, 0:1] * o_lv[3, 0:1]
+        f1 = 1.0 - f0
+        fwd.wait_recv()
+        own_lone = [f0 * o_lv[j, 1:2] + f1 * o_lv[j, 0:1] for j in range(DP)]
+        lone = None
+        for j in range(DP):
+            a = inb[pl.ds(256 * j, TOK)].astype(F32)
+            b = inb[pl.ds(256 * j + TOK, TOK)].astype(F32)
+            o_x[pl.ds(ROWS * j, TOK)] = (f0 * a + f1 * b).astype(BF16)
+            term = own_lone[j] * (f0 * b + f1 * a)
+            lone = term if lone is None else lone + term
+        lone = lone.astype(BF16)
+        for j in range(DP):
+            o_x[pl.ds(ROWS * j + TOK, PART)] = lone[PART * j : PART * (j + 1)]
+        for c in qw:
+            c.wait_recv()
+        project(chip_rows(0))
+        project(chip_rows(1))
+    else:
+        for c in qw:
+            c.wait_recv()
+        project(chip_rows(L.x))
+        fwd.wait_recv()
+        project(chip_rows(1 - L.x))
+
+    pack_pairs(qx, sbq)
+    o_qkv[token_rows(s)] = sbq[s]
+    qc = [L.copy(sbq.at[p], o_qkv.at[token_rows(s)], (d, p)) for p in L.seq_peers]
+    gw = [L.copy(wg.at[:, c], o_wg.at[own], (p, s)) for p, c in zip(L.dp_peers, cols)]
+    gw += [L.copy(wu.at[:, c], o_wu.at[own], (p, s)) for p, c in zip(L.dp_peers, cols)]
+    if first:
+        cbuf[d] = cot[:, token_part(d), :]
+        cc = [L.copy(cot.at[:, token_part(p), :], cbuf.at[d], (p, s)) for p in L.dp_peers]
+    for c in qc:
+        c.wait_recv()
+
+    keep = low_lanes((LEN, 128))
+    k = o_qkv[:, pl.ds(128, 128)].astype(F32)
+    kz[0] = jnp.where(keep, k, 0.0).astype(BF16)
+    kz[1] = jnp.where(keep, 0.0, k).astype(BF16)
+
+    @pl.loop(0, LEN // QB)
+    def _(i):
+        at = pl.ds(pl.multiple_of(i * QB, QB), QB)
+        q = o_qkv[at, pl.ds(0, 128)]
+        outs, logs = [], []
+        for j in range(2):
+            sc = mm_t(q, kz[j])
+            top = jnp.max(sc, axis=-1, keepdims=True)
+            ex = jnp.exp(sc - top)
+            tot = jnp.sum(ex, axis=-1, keepdims=True)
+            o = mm(ex.astype(BF16), o_qkv[:, pl.ds(256, 128)])
+            outs.append(o / tot)
+            logs.append(jnp.broadcast_to(top + jnp.log(tot), (QB, 128)))
+        pick = low_lanes((QB, 128))
+        ctx = jnp.where(pick, outs[0], outs[1])
+        o_ctx[at] = ctx
+        o_lse[at] = jnp.where(pick, logs[0], logs[1])
+        cbk[at] = ctx.astype(BF16)
+
+    crx[s] = cbk[token_rows(s)]
+    bc = [L.copy(cbk.at[token_rows(p)], crx.at[s], (d, p)) for p in L.seq_peers]
+    if first:
+        for c in cc:
+            c.wait_recv()
+        a = cot[0].astype(F32)
+        b = cot[1].astype(F32)
+        o_cot[pl.ds(0, TOK)] = f0 * a + f1 * b
+        lone = None
+        for j in range(DP):
+            term = own_lone[j] * (f0 * cbuf[j, 1].astype(F32) + f1 * cbuf[j, 0].astype(F32))
+            lone = term if lone is None else lone + term
+        o_cot[pl.ds(TOK, PART)] = lone
+    for c in bc:
+        c.wait_recv()
+    unpack_pairs(crx, o_ce)
+
+    for c in (1 - L.x, L.x):
+        rows = chip_rows(c)
+        part[rows] = mm(o_ce[rows], o_wo[...])
+    c_other = reduce_other(L, part, red_a)
+    c_own = reduce_own(L, part, red_a)
+    c_cross = reduce_cross(L, part, red_a, c_other)
+    attn = reduce_end(L, part, red_a, c_own, c_cross)
+    if first:
+        res = block(o_x, d)[...].astype(F32) + attn
+    else:
+        res = hin[...] + attn
+    base = 4 * layer
+    xhat, rstd = normalize(res)
+    norm_a = xhat * nv[base : base + 1] + nv[base + 1 : base + 2]
+    block(o_actf, d)[...] = norm_a.astype(BF16)
+    near, far = gather_begin(L, o_actf)
+    o_xa[...] = xhat
+    o_ra[...] = jnp.broadcast_to(rstd, (ROWS, 128))
+    for c in loc:
+        c.wait()
+    for c in gw:
+        c.wait_recv()
+
+    def feed(rows):
+        a = o_actf[rows]
+        gp = mm(a, o_wg[...])
+        up = mm(a, o_wu[...])
+        o_gp[rows] = gp
+        o_up[rows] = up
+        hid = (gp * jax.nn.sigmoid(gp) * up).astype(BF16)
+        o_hid[rows] = hid
+        part[rows] = mm(hid, wd[...])
+
+    near.wait_recv()
+    feed(chip_rows(L.x))
+    c_own = reduce_own(L, part, red_f)
+    fwd = gather_forward(L, o_actf, far)
+    fwd.wait_recv()
+    feed(chip_rows(1 - L.x))
+    c_other = reduce_other(L, part, red_f)
+    c_cross = reduce_cross(L, part, red_f, c_other)
+    res = norm_a + reduce_end(L, part, red_f, c_own, c_cross)
+    xhat, rstd = normalize(res)
+    o_h[...] = xhat * nv[base + 2 : base + 3] + nv[base + 3 : base + 4]
+    o_xf[...] = xhat
+    o_rf[...] = jnp.broadcast_to(rstd, (ROWS, 128))
+    L.drain()
+
+
+def token_part(p):
+    return pl.ds(pl.multiple_of(p * PART, PART), PART)
+
+
+def backward_kernel(layer, *refs):
+    (gin, nv, x, qkv, lse, ctx, ce, actf, gp, up, hid, xa, xf, ra, rf, wq, wg, wu, wo, wd, cosf, sinf, v_in) = refs[:23]
+    (o_g, o_w, o_v) = refs[23:26]
+    (part, db, dg, du, dsb, dc, sbq, dback, drx, dqkv, kz, vz, kt, lt, et, dkv, dqt) = refs[26:43]
+    red_f, red_a = refs[43:47], refs[47:51]
+    send, recv = refs[51:53]
+    L = Links(send, recv)
+    L.enter([(p, L.s) for p in (L.xp, L.sib)] + [(L.d, p) for p in L.seq_peers])
+    d, s = L.d, L.s
+    base = 4 * layer
+
+    o_v[...] = v_in[...]
+    grad = gin[...]
+    xhat = xf[...]
+    d_res_f = normalize_back(grad, nv[base + 2 : base + 3], xhat, rf[:, 0:1])
+    block(db, d)[...] = d_res_f.astype(BF16)
+    near, far = gather_begin(L, db)
+    o_v[base + 2 : base + 3] = jnp.sum(grad * xhat, axis=0, keepdims=True)
+    o_v[base + 3 : base + 4] = jnp.sum(grad, axis=0, keepdims=True)
+
+    def feed(rows):
+        dh = mm_t(db[rows], wd[...])
+        g, u = gp[rows], up[rows]
+        sig = jax.nn.sigmoid(g)
+        dgv = (dh * u * sig * (1.0 + g * (1.0 - sig))).astype(BF16)
+        duv = (dh * g * sig).astype(BF16)
+        dg[rows] = dgv
+        du[rows] = duv
+        part[rows] = mm_t(dgv, wg[...]) + mm_t(duv, wu[...])
+
+    near.wait_recv()
+    feed(chip_rows(L.x))
+    c_own = reduce_own(L, part, red_f)
+    fwd = gather_forward(L, db, far)
+    fwd.wait_recv()
+    feed(chip_rows(1 - L.x))
+    c_other = reduce_other(L, part, red_f)
+    c_cross = reduce_cross(L, part, red_f, c_other)
+    quarter = D // DP
+    o_w[pl.ds(12, 4)] = t_mm(hid[...], db[...]).astype(BF16).reshape(4, quarter, D)
+    o_w[pl.ds(4, 4)] = t_mm(actf[...], dg[...]).astype(BF16).reshape(4, quarter, D)
+    o_w[pl.ds(8, 4)] = t_mm(actf[...], du[...]).astype(BF16).reshape(4, quarter, D)
+    d_norm = d_res_f + reduce_end(L, part, red_f, c_own, c_cross)
+    xhat = xa[...]
+    d_res_a = normalize_back(d_norm, nv[base : base + 1], xhat, ra[:, 0:1])
+
+    block(dsb, d)[...] = d_res_a.astype(BF16)
+    near, far = gather_begin(L, dsb)
+    o_v[base : base + 1] = jnp.sum(d_norm * xhat, axis=0, keepdims=True)
+    o_v[base + 1 : base + 2] = jnp.sum(d_norm, axis=0, keepdims=True)
+    fwd = gather_forward(L, dsb, far)
+    near.wait_recv()
+    fwd.wait_recv()
+    dg[:, pl.ds(0, 256)] = mm_t(dsb[...], wo[...]).astype(BF16)
+    pack_pairs(dg.at[:, pl.ds(0, 256)], sbq)
+    dc[token_rows(s)] = sbq[s]
+    qc = [L.copy(sbq.at[p], dc.at[token_rows(s)], (d, p)) for p in L.seq_peers]
+
+    g_out = t_mm(ce[...], dsb[...])
+    o_w[16, pl.ds(0, 128)] = g_out[0:128].astype(BF16)
+    o_w[16, pl.ds(128, 64)] = (g_out[128:192] + g_out[192:256]).astype(BF16)
+
+    keep = low_lanes((LEN, 128))
+    k = qkv[:, pl.ds(128, 128)].astype(F32)
+    kz[0] = jnp.where(keep, k, 0.0).astype(BF16)
+    kz[1] = jnp.where(keep, 0.0, k).astype(BF16)
+    kt[0] = kz[0].astype(F32).T.astype(BF16)
+    kt[1] = kz[1].astype(F32).T.astype(BF16)
+    v = qkv[:, pl.ds(256, 128)].astype(F32)
+    vz[0] = jnp.where(keep, v, 0.0).astype(BF16)
+    vz[1] = jnp.where(keep, 0.0, v).astype(BF16)
+    lt[...] = lse[...].T
+    for c in qc:
+        c.wait_recv()
+    et[...] = (dc[...].astype(F32) * ctx[...]).T
+    dkv[...] = jnp.zeros_like(dkv)
+    pick = low_lanes((QB, 128))
+
+    @pl.loop(0, LEN // QB)
+    def _(i):
+        at = pl.ds(pl.multiple_of(i * QB, QB), QB)
+        q = qkv[at, pl.ds(0, 128)]
+        g = dc[at]
+        qf, gf = q.astype(F32), g.astype(F32)
+        acc = None
+        for j in range(2):
+            qz = (jnp.where(pick, qf, 0.0) if j == 0 else jnp.where(pick, 0.0, qf)).astype(BF16)
+            gz = (jnp.where(pick, gf, 0.0) if j == 0 else jnp.where(pick, 0.0, gf)).astype(BF16)
+            log = lt[pl.ds(64 * j, 1), at]
+            inner = jnp.sum(et[pl.ds(64 * j, 64), at], axis=0, keepdims=True)
+            pr = jnp.exp(mm_t(kz[j], q) - log)
+            dp = mm_t(vz[j], g)
+            ds = (pr * (dp - inner)).astype(BF16)
+            dkv[:, pl.ds(128, 128)] += mm(pr.astype(BF16), gz)
+            dkv[:, pl.ds(0, 128)] += mm(ds, qz)
+            term = mm(kt[j], ds)
+            acc = term if acc is None else acc + term
+        dqt[:, at] = acc
+
+    def unrotate(g):
+        return g * cosf[...] - swap_halves(g) * sinf[...]
+
+    dback[:, pl.ds(0, 128)] = unrotate(dqt[...].T * (HEAD**-0.5)).astype(BF16)
+    dback[:, pl.ds(128, 128)] = unrotate(dkv[:, pl.ds(0, 128)]).astype(BF16)
+    dback[:, pl.ds(256, 128)] = dkv[:, pl.ds(128, 128)].astype(BF16)
+    drx[s] = dback[token_rows(s)]
+    bc = [L.copy(dback.at[token_rows(p)], drx.at[s], (d, p)) for p in L.seq_peers]
+    for c in bc:
+        c.wait_recv()
+    unpack_pairs(drx, dqkv)
+    for c in (1 - L.x, L.x):
+        rows = chip_rows(c)
+        part[rows] = mm_t(dqkv[rows], wq[...])
+    c_other = reduce_other(L, part, red_a)
+    c_own = reduce_own(L, part, red_a)
+    c_cross = reduce_cross(L, part, red_a, c_other)
+    o_w[pl.ds(0, 4)] = t_mm(x[...], dqkv[...]).astype(BF16).reshape(4, quarter, D)
+    o_g[...] = d_res_a + reduce_end(L, part, red_a, c_own, c_cross)
+    L.drain()
+
+
+BLOCKS = 17
+CHUNKS = [(0, 4), (4, 4), (8, 4), (12, 5)]
+ZS = 4
+ZR = D // DP // ZS
+YC = D // 2
+
+
+def reduce_kernel(*refs):
+    (w1, w2, vin, lone) = refs[:4]
+    (f1, f2, o_v, o_lone) = refs[4:8]
+    bufs = [refs[8:12], refs[12:16]]
+    (vy, vz, vs, vx, va, vb, vc) = refs[16:23]
+    send, recv = refs[23:25]
+    L = Links(send, recv)
+    d, s, y, z = L.d, L.s, L.y, L.z
+    yp = 2 * z + (1 - y)
+    zps = [lax.rem(z + k, ZS) for k in range(1, ZS)]
+    zdev = [(d, 2 * p + y) for p in zps]
+    L.enter([(p, s) for p in L.dp_peers] + [(d, yp)] + zdev)
+    mine = pl.ds(pl.multiple_of(y * YC, 128), YC)
+    theirs = pl.ds(pl.multiple_of((1 - y) * YC, 128), YC)
+    zrows = pl.ds(pl.multiple_of(z * ZR, ZR), ZR)
+
+    o_lone[d] = lone[...]
+    lc = [L.copy(lone, o_lone.at[d], (p, s)) for p in L.dp_peers]
+    vcp = L.copy(vin, vy, (d, yp))
+    jobs = []
+    for w, f, (ry, h, rz, sm) in ((w2, f2, bufs[1]), (w1, f1, bufs[0])):
+        for at, n in CHUNKS:
+            jobs.append((w, f, ry, h, rz, sm, at, n))
+    ys = [L.copy(w.at[pl.ds(at, n), :, theirs], ry.at[pl.ds(at, n)], (d, yp)) for (w, f, ry, h, rz, sm, at, n) in jobs]
+    vcp.wait_recv()
+    va[...] = vin[...] + vy[...]
+    vzc = [L.copy(va, vz.at[k], zdev[k]) for k in range(ZS - 1)]
+    zs = []
+    for c, (w, f, ry, h, rz, sm, at, n) in zip(ys, jobs):
+        r = pl.ds(at, n)
+        c.wait_recv()
+        h[r] = (w[r, :, mine].astype(F32) + ry[r].astype(F32)).astype(BF16)
+        zs.append(
+            [
+                L.copy(h.at[r, pl.ds(pl.multiple_of(zps[k] * ZR, ZR), ZR)], rz.at[k, r], zdev[k])
+                for k in range(ZS - 1)
+            ]
+        )
+    for c in vzc:
+        c.wait_recv()
+    vb[...] = va[...] + vz[0] + vz[1] + vz[2]
+    vsc = L.copy(vb, vs, (L.sib, s))
+    ds = []
+    for cs, (w, f, ry, h, rz, sm, at, n) in zip(zs, jobs):
+        r = pl.ds(at, n)
+        for c in cs:
+            c.wait_recv()
+        total = h[r, zrows].astype(F32)
+        for k in range(ZS - 1):
+            total = total + rz[k, r].astype(F32)
+        if n == 4:
+            sm[r] = total.astype(BF16)
+            f[y, at + d, zrows] = sm[at + d]
+            ds.append([L.copy(sm.at[at + p], f.at[y, at + d, zrows], (p, s)) for p in L.dp_peers])
+        else:
+            f[y, r, zrows] = total.astype(BF16)
+            ds.append([])
+    vsc.wait_recv()
+    vc[...] = vb[...] + vs[...]
+    vxc = L.copy(vc, vx, (L.xp, s))
+    gs = []
+    for cs, (w, f, ry, h, rz, sm, at, n) in zip(ds, jobs):
+        r = pl.ds(at, n)
+        for c in cs:
+            c.wait_recv()
+        gs.append([L.copy(f.at[y, r, zrows], f.at[y, r, zrows], p) for p in zdev])
+    es = []
+    for cs, (w, f, ry, h, rz, sm, at, n) in zip(gs, jobs):
+        r = pl.ds(at, n)
+        for c in cs:
+            c.wait_recv()
+        es.append(L.copy(f.at[y, r], f.at[y, r], (d, yp)))
+    for c in es + lc:
+        c.wait_recv()
+    vxc.wait_recv()
+    o_v[...] = vc[...] + vx[...]
+    L.drain()
+
+
+def sds(shape, dtype):
+    return jax.ShapeDtypeStruct(shape, dtype)
+
+
+def call(body, name, cid, outs, scratch, flops, args, anyargs=()):
+    return pl.pallas_call(
+        body,
+        name=name,
+        out_shape=[sds(*o) for o in outs],
+        in_specs=[
+            pl.BlockSpec(memory_space=pl.ANY if i in anyargs else pltpu.VMEM) for i in range(len(args))
+        ],
+        out_specs=[pl.BlockSpec(memory_space=pltpu.VMEM)] * len(outs),
+        scratch_shapes=scratch,
+        cost_estimate=pl.CostEstimate(flops=flops, bytes_accessed=2 * 10**7, transcendentals=10**6),
+        compiler_params=pltpu.CompilerParams(
+            collective_id=cid, has_side_effects=True, vmem_limit_bytes=58 * 2**20
+        ),
+    )(*args)
+
+
+SAVED = [
+    ((ALL, D), BF16),
+    ((LEN, 384), BF16),
+    ((LEN, 128), F32),
+    ((LEN, 128), F32),
+    ((ALL, 256), BF16),
+    ((ALL, D), BF16),
+    ((ALL, D), F32),
+    ((ALL, D), F32),
+    ((ALL, D), BF16),
+    ((ROWS, D), F32),
+    ((ROWS, D), F32),
+    ((ROWS, 128), F32),
+    ((ROWS, 128), F32),
+    ((D, D), BF16),
+    ((D, D), BF16),
+    ((D, D), BF16),
+    ((256, D), BF16),
+]
+
+
+def run_forward(first, layer, args, anyargs):
+    outs = [((ROWS, D), F32)] + SAVED
+    scratch = []
+    if first:
+        outs = outs + [((ROWS, D), F32), ((DP, 8, D), F32), ((8, D), F32)]
+        scratch = [
+            pltpu.VMEM((DP * 256, D), BF16),
+            pltpu.VMEM((DP, 2, PART, D), BF16),
+            pltpu.VMEM((DP, 8, D), F32),
+        ]
+    scratch = scratch + [
+        pltpu.VMEM((ALL, D), F32),
+        pltpu.VMEM((ALL, D), BF16),
+        pltpu.VMEM((SQ, TOK, 384), BF16),
+        pltpu.VMEM((LEN, 128), BF16),
+        pltpu.VMEM((SQ, TOK, 128), BF16),
+        pltpu.VMEM((2, LEN, 128), BF16),
+    ]
+    scratch = scratch + REDUCE_BUFS + REDUCE_BUFS
+    scratch += [pltpu.SemaphoreType.DMA((64,)), pltpu.SemaphoreType.DMA((64,)), pltpu.SemaphoreType.DMA((2,))]
+    body = functools.partial(forward_kernel, first, layer)
+    return call(body, "fwd" + str(layer), 1 + layer, outs, scratch, 6 * 10**9, args, anyargs)
+
+
+def run_backward(layer, args):
+    outs = [((ROWS, D), F32), ((BLOCKS, D // DP, D), BF16), ((8, D), F32)]
+    scratch = [
+        pltpu.VMEM((ALL, D), F32),
+        pltpu.VMEM((ALL, D), BF16),
+        pltpu.VMEM((ALL, D), BF16),
+        pltpu.VMEM((ALL, D), BF16),
+        pltpu.VMEM((ALL, D), BF16),
+        pltpu.VMEM((LEN, 128), BF16),
+        pltpu.VMEM((SQ, TOK, 128), BF16),
+        pltpu.VMEM((LEN, 384), BF16),
+        pltpu.VMEM((SQ, TOK, 384), BF16),
+        pltpu.VMEM((ALL, D), BF16),
+        pltpu.VMEM((2, LEN, 128), BF16),
+        pltpu.VMEM((2, LEN, 128), BF16),
+        pltpu.VMEM((2, 128, LEN), BF16),
+        pltpu.VMEM((128, LEN), F32),
+        pltpu.VMEM((128, LEN), F32),
+        pltpu.VMEM((LEN, 256), F32),
+        pltpu.VMEM((128, LEN), F32),
+    ]
+    scratch = scratch + REDUCE_BUFS + REDUCE_BUFS
+    scratch += [pltpu.SemaphoreType.DMA((64,)), pltpu.SemaphoreType.DMA((64,))]
+    body = functools.partial(backward_kernel, layer)
+    return call(body, "bwd" + str(layer), 3 + layer, outs, scratch, 12 * 10**9, args)
+
+
+def run_reduce(args):
+    quarter = D // DP
+    outs = [((2, BLOCKS, quarter, YC), BF16)] * 2 + [((8, D), F32), ((DP, 2, PART, D), BF16)]
+    one = [
+        pltpu.VMEM((BLOCKS, quarter, YC), BF16),
+        pltpu.VMEM((BLOCKS, quarter, YC), BF16),
+        pltpu.VMEM((ZS - 1, BLOCKS, ZR, YC), BF16),
+        pltpu.VMEM((12, ZR, YC), BF16),
+    ]
+    row = pltpu.VMEM((8, D), F32)
+    scratch = one + one + [row, pltpu.VMEM((ZS - 1, 8, D), F32)] + [row] * 5
+    scratch += [pltpu.SemaphoreType.DMA((128,)), pltpu.SemaphoreType.DMA((128,))]
+    return call(reduce_kernel, "wsum", 5, outs, scratch, 10**8, args)
+
+
+def spread_qkv(w):
+    depth = w.shape[0]
+    w = w.reshape(depth, 3, DP, 192).transpose(2, 0, 1, 3)
+    pair = w[..., :128].reshape(DP, depth, 384)
+    third = w[..., 128:]
+    third = jnp.concatenate([third, third], axis=-1).reshape(DP, depth, 384)
+    return jnp.concatenate([pair, third], axis=-1)
+
+
+def rotary():
+    half = HEAD // 2
+    freqs = 1000.0 ** (-(jnp.arange(half).astype(F32) * 2.0 / HEAD))
+    angles = jnp.arange(LEN).astype(F32)[:, None] * freqs[None, :]
+    co, si = jnp.cos(angles), jnp.sin(angles)
+    return jnp.concatenate([co] * 4, axis=1), jnp.concatenate([-si, si, -si, si], axis=1)
+
+
+def own_rows(table, s):
+    mine = lax.dynamic_slice_in_dim(table, s * TOK, TOK, 0)
+    parts = []
+    for j in range(DP):
+        parts += [mine, mine[PART * j : PART * (j + 1)]]
+    return jnp.concatenate(parts, axis=0)
+
+
+def final_grads(f):
+    f = f.astype(F32)
+    quarter = D // DP
+    pair = f[0, 0:4].reshape(DP, quarter, 3, 128)
+    third = f[1, 0:4].reshape(DP, quarter, 3, 2, 64).sum(axis=3)
+    g_qkv = jnp.concatenate([pair, third], axis=-1).transpose(1, 2, 0, 3).reshape(quarter, 3 * D)
+    g_gate = f[:, 4:8].transpose(2, 1, 0, 3).reshape(quarter, DP * D)
+    g_up = f[:, 8:12].transpose(2, 1, 0, 3).reshape(quarter, DP * D)
+    g_down = f[:, 12:16].transpose(1, 2, 0, 3).reshape(D, D)
+    g_out = f[:, 16].transpose(1, 0, 2).reshape(quarter, D)
+    return g_qkv, g_out, g_gate, g_up, g_down
+
+
+def shared_device(inputs, cotangent, live, *weights):
+    sets = (weights[:9], weights[9:])
+    d, s = lax.axis_index("dp"), lax.axis_index("seq")
+    cosf, sinf = rotary()
+    cosr, sinr = own_rows(cosf, s), own_rows(sinf, s)
+    livet = jnp.broadcast_to(jnp.pad(live[:, 0].astype(F32), (0, 6))[:, None], (8, D))
+    norms = jnp.stack([sets[i][j] for i in range(2) for j in (2, 3, 7, 8)]).astype(F32)
+    norms = lax.dynamic_update_slice(jnp.zeros((8, D), F32), norms, (0, d * (D // DP)))
+    sends = [spread_qkv(w[0]) for w in sets]
+
+    args = (inputs[:, 0], livet, cotangent[:, 0], norms, sends[0], sets[0][4], sets[0][5], sets[0][1], sets[0][6], cosr, sinr)
+    res = run_forward(True, 0, args, (5, 6))
+    h1, saved1 = res[0], res[1:18]
+    gcot, lv, nv = res[18:]
+    args = (h1, nv, sends[1], sets[1][4], sets[1][5], sets[1][1], sets[1][6], cosr, sinr)
+    res = run_forward(False, 1, args, (3, 4))
+    h2, saved2 = res[0], res[1:18]
+    g, w2, v2 = run_backward(1, (gcot, nv) + tuple(saved2) + (sets[1][6], cosf, sinf, jnp.zeros((8, D), F32)))
+    g, w1, v1 = run_backward(0, (g, nv) + tuple(saved1) + (sets[0][6], cosf, sinf, v2))
+    out_rows = h2.astype(BF16)
+    in_rows = g.astype(BF16)
+    f1, f2, vsum, lone = run_reduce((w1, w2, v1, jnp.stack([out_rows[TOK:], in_rows[TOK:]])))
+
+    full0 = lv[:, 0, 0].min() > 0.5
+    here = jnp.where(full0, live[1, 0], live[0, 0]) > 0
+
+    def place(rows, k):
+        part = lone[:, k].reshape(TOK, D)
+        part = jnp.where(here, part, jnp.zeros_like(part))
+        whole = rows[:TOK]
+        return jnp.stack([jnp.where(full0, whole, part), jnp.where(full0, part, whole)])[:, None]
+
+    vsum = lax.dynamic_slice_in_dim(vsum, d * (D // DP), D // DP, 1)
+    out = [place(out_rows, 0), place(in_rows, 1)]
+    for i, f in enumerate((f1, f2)):
+        g_qkv, g_out, g_gate, g_up, g_down = final_grads(f)
+        v = vsum[4 * i : 4 * i + 4]
+        out += [g_qkv, g_out, v[0], v[1], g_gate, g_up, g_down, v[2], v[3]]
+    return tuple(out)
+
+
+def fits(mesh):
+    return mesh.shape["dp"] == DP and mesh.shape["seq"] == SQ
 
 
 def as_sent(array):
@@ -294,8 +1068,13 @@
 
 
 def solution(mesh):
+    def device(inputs, cotangent, *rest):
+        if fits(mesh) and inputs.shape == (2, 1, TOK, D):
+            return shared_device(inputs, cotangent, *rest)
+        return per_device(inputs, cotangent, *rest)
+
     return jax.shard_map(
-        per_device,
+        device,
         mesh=mesh,
         in_specs=(
             P(None, "dp", "seq", None),

time: 2100 us -> 751 us (0.36)
  waiting for transfers between devices: 1610 us -> 0 us
  Pallas kernels: 0 us -> 628 us
  matrix products: 219 us -> 0 us
  other arithmetic: 78.2 us -> 25.6 us
  blocking collectives: 46.3 us -> 0 us
  local copies, waits for them, and re-layouts: 113 us -> 81.5 us
    pallas_call x0 -> x5, Pallas kernels: none -> 628 us  [call(): pl.pallas_call(body, name=name, out_shape=[sds(*o) for o in outs], in_spe...]
    all_gather x18 -> x0, waiting for transfers between devices: 561 us -> none  [the longest x10 283 us: per_device(): full = lax.all_gather(as_sent(local_sets[index]), 'dp', axis=0, tiled=True)]
    unnamed x46 -> x0, waiting for transfers between devices: 405 us -> none
    reduce_scatter x9 -> x0, waiting for transfers between devices: 393 us -> none  [per_device(): lax.psum_scatter(as_sent(totals[index]), 'dp', scatter_dimension=0, tiled...]
    psum x1 -> x0, waiting for transfers between devices: 248 us -> none  [per_device(): lax.psum(as_sent(shares), 'seq')]
    dot_general x84 -> x0, matrix products: 219 us -> none  [the longest x20 48.6 us: dot_first(): lax.dot_general(left, right, (((0,), (0,)), ((), ())), preferred_element_...]
    unnamed x608 -> x30, local copies, waits for them, and re-layouts: 92.8 us -> 4.83 us
    convert_element_type x41 -> x7, other arithmetic: 43.3 us -> 10.1 us  [the longest x2 7.31 us: final_grads(): f = f.astype(F32)]
  transfers between devices with their start and end apart: 37 -> 0, of which waited for: 36 -> 0; matrix products, arithmetic and copies ran while one was open for 15% -> 0% of each run, Pallas kernels for 0% -> 0%
where the time goes in v1:
time: 751 us; the launch traced here: 739 us
  Pallas kernels  628 us (84%)
  local copies, waits for them, and re-layouts  81.5 us (11%)
  other arithmetic  25.6 us (3%)
    pallas_call x5, Pallas kernels, call(): pl.pallas_call(body, name=name, out_shape=[sds(*o) for o in outs], in_spe...  628 us

profile of v1, /device:TPU:10, one launch (start us, length us, event | category | flops | bytes accessed | tf_op | source)
XLA Modules:
  0.0 738.8 jit_solution(17816152324951001240)
XLA Ops:
  0.7 0.7 convert_bitcast_fusion
  1.3 0.7 stack.54
  2.0 0.7 stack.55
  2.7 0.7 stack.56
  3.3 0.7 stack.57
  4.0 0.7 stack.58
  4.6 0.7 stack.59
  5.3 0.7 stack.60
  6.0 0.7 stack.61
  6.6 1.3 fusion.4
  8.0 0.7 broadcast_in_dim.6.refs_1_
  8.8 2.9 reshape.107
  13.4 1.1 pad_maximum_fusion.2
  15.1 1.1 pad_maximum_fusion.refs_4_
  16.2 1.1 reshape.110
  19.0 1.1 pad_maximum_fusion.3
  20.1 1.0 reshape.112
  21.1 1.1 pad_maximum_fusion.1.refs_2_
  22.2 1.9 fusion
  24.1 0.9 pad_maximum_fusion.4
  25.4 0.7 copy-done.4
  26.1 0.7 copy-done.5
  26.8 96.7 %fwd0.1 = (f32[160,768]{1,0:T(8,128)}, bf16[640,768]{1,0:T(8,128)(2,1)}, bf16[1024,384]{1,0:T(8,128)(2,1)}, f32[1024,128]{1,0:T(8,128)}, f32[1024,128]{1,0:T(8,1...) custom-call(bf16[2,128,768]{2,1,0:T(8,128)(2,1)} %bitcast.106, ...), custom_call_target="tpu_custom_call" | custom-call | flops 6000000000 | bytes 20000000 | tf_op jit(solution)/shard_map/fwd0/pallas_call | solution.py:597
  123.5 1.3 slice_reduce_fusion
  126.8 88.5 %fwd1.1 = (f32[160,768]{1,0:T(8,128)}, bf16[640,768]{1,0:T(8,128)(2,1)}, bf16[1024,384]{1,0:T(8,128)(2,1)}, f32[1024,128]{1,0:T(8,128)}, f32[1024,128]{1,0:T(8,1...) custom-call(f32[160,768]{1,0:T(8,128)} %get-tuple-element.70.refs_0_, ...), custom_call_target="tpu_custom_call" | custom-call | flops 6000000000 | bytes 20000000 | tf_op jit(solution)/shard_map/fwd1/pallas_call | solution.py:597
  215.3 1.1 convert_element_type.70
  217.0 76.6 %bwd1.1 = (f32[160,768]{1,0:T(8,128)}, bf16[17,192,768]{2,1,0:T(8,128)(2,1)}, f32[8,768]{1,0:T(8,128)}) custom-call(f32[160,768]{1,0:T(8,128)} %get-tuple-element.73.refs_0_, f32[8,768]{1,0:T(8,128)} %get-tuple-element.71.refs_1_, bf16[640,768]{1,0:T(8,128)(2,1)} %get-tuple-element.74.refs_2_, bf16[1024,384]{1,0:T(8,128)(2,1)} %get-tuple-element.75.refs_3_, ...), custom_call_target="tpu_custom_call" | custom-call | flops 12000000000 | bytes 20000000 | tf_op jit(solution)/shard_map/bwd1/pallas_call | solution.py:597
  293.6 78.3 %bwd0.1 = (f32[160,768]{1,0:T(8,128)}, bf16[17,192,768]{2,1,0:T(8,128)(2,1)}, f32[8,768]{1,0:T(8,128)}) custom-call(f32[160,768]{1,0:T(8,128)} %get-tuple-element.91.refs_0_, f32[8,768]{1,0:T(8,128)} %get-tuple-element.71.refs_1_, bf16[640,768]{1,0:T(8,128)(2,1)} %get-tuple-element.92.refs_2_, bf16[1024,384]{1,0:T(8,128)(2,1)} %get-tuple-element.93.refs_3_, ...), custom_call_target="tpu_custom_call" | custom-call | flops 12000000000 | bytes 20000000 | tf_op jit(solution)/shard_map/bwd0/pallas_call | solution.py:597
  372.0 1.1 convert_element_type.71
  373.7 288.2 %wsum.1 = (bf16[2,17,192,384]{3,2,1,0:T(8,128)(2,1)}, bf16[2,17,192,384]{3,2,1,0:T(8,128)(2,1)}, f32[8,768]{1,0:T(8,128)}, bf16[4,2,32,768]{3,2,1,0:T(8,128)(2,1)}) custom-call(bf16[17,192,768]{2,1,0:T(8,128)(2,1)} %get-tuple-element.110.refs_0_, bf16[17,192,768]{2,1,0:T(8,128)(2,1)} %get-tuple-element.111.refs_1_, f32[8,768]{1,0:T(8,128)} %get-tuple-element.112.refs_2_, ...), custom_call_target="tpu_custom_call" | custom-call | flops 100000000 | bytes 20000000 | tf_op jit(solution)/shard_map/wsum/pallas_call | solution.py:597
  661.9 1.1 slice_select_fusion
  663.1 0.8 maximum_bitcast_fusion.2
  663.8 0.8 maximum_bitcast_fusion.3
  664.6 1.9 fusion.3
  666.5 2.4 fusion.2
  669.4 1.7 copy.98
  671.2 1.1 reduce_sum.18
  672.3 1.6 copy.99
  673.9 0.8 maximum_bitcast_fusion
  674.7 1.5 copy.100
  676.2 2.8 reshape.113
  679.0 2.4 fusion.1
  681.9 1.7 copy.105
  683.6 1.1 reduce_sum.19
  684.7 2.0 copy.106
  686.8 0.8 maximum_bitcast_fusion.1
  687.5 1.5 copy.107
  689.1 2.8 reshape.118
  691.8 3.7 convert_element_type.73
  696.2 1.8 copy.111
  698.0 1.6 copy.117
  699.6 0.9 copy.115
  700.4 3.2 copy.109
  703.6 4.3 reshape.120
  707.9 3.2 copy.110
  711.1 4.1 reshape.121
  715.3 3.7 convert_element_type.72
  719.6 1.8 copy.104
  721.5 1.6 copy.116
  723.0 0.9 copy.114
  723.9 3.2 copy.102
  727.1 4.1 reshape.115
  731.2 3.2 copy.103
  734.5 4.1 reshape.116
  (54 shorter events, 8.1 us)
Async XLA Ops:
  8.8 3.5 copy-start.3
  14.5 1.7 copy-start.2
  25.0 98.5 %copy-start = (f32[1024,128]{1,0:T(8,128)}, f32[1024,128]{1,0:T(8,128)S(1)}, u32[]{:S(2)}) copy-start(f32[1024,128]{1,0:T(8,128)S(1)} %get-tuple-element.247.refs_20_) | copy-start | bytes 1572868
  25.0 98.5 %copy-start.1 = (f32[1024,128]{1,0:T(8,128)}, f32[1024,128]{1,0:T(8,128)S(1)}, u32[]{:S(2)}) copy-start(f32[1024,128]{1,0:T(8,128)S(1)} %get-tuple-element.248.refs_21_) | copy-start | bytes 1572868
  25.2 0.9 copy-start.4
  26.1 0.7 copy-start.5

commit v2 on v0

--- a/solution.py
+++ b/solution.py
@@ -1,9 +1,1277 @@
+import functools
+
 import jax
 import jax.numpy as jnp
+import numpy as np
 from jax import lax
+from jax.experimental import pallas as pl
+from jax.experimental.pallas import tpu as pltpu
 from jax.sharding import PartitionSpec as P
 
 HEAD = 64
+
+DP = 4
+SQ = 8
+TOK = 128
+PART = TOK // DP
+ROWS = TOK + PART
+ALL = DP * ROWS
+HALF = 2 * ROWS
+D = 768
+LEN = SQ * TOK
+QB = 256
+F32 = jnp.float32
+BF16 = jnp.bfloat16
+VMEM_LIMIT = 64 * 2**20
+MESH = pl.DeviceIdType.MESH
+
+
+def mm(a, b):
+    return lax.dot_general(a, b, (((1,), (0,)), ((), ())), preferred_element_type=F32)
+
+
+def mm_t(a, b):
+    return lax.dot_general(a, b, (((1,), (1,)), ((), ())), preferred_element_type=F32)
+
+
+def t_mm(a, b):
+    return lax.dot_general(a, b, (((0,), (0,)), ((), ())), preferred_element_type=F32)
+
+
+def low_lanes(shape):
+    return lax.rem(lax.broadcasted_iota(jnp.int32, shape, len(shape) - 1), 128) < 64
+
+
+def swap_halves(x):
+    lane = lax.broadcasted_iota(jnp.int32, x.shape, 1)
+    return jnp.where(lax.rem(lane, 64) < 32, pltpu.roll(x, 96, 1), pltpu.roll(x, 32, 1))
+
+
+def flip(x):
+    return pltpu.roll(x, 64, 1)
+
+
+class Links:
+    def __init__(self, send, recv, lsem):
+        self.send, self.recv, self.used, self.sent, self.slow = send, recv, 0, [], []
+        self.lsem, self.locals_used = lsem, 0
+        self.d = lax.axis_index("dp")
+        self.s = lax.axis_index("seq")
+        self.x = self.d // 2
+        self.core = lax.rem(self.d, 2)
+        self.sib = 2 * self.x + (1 - self.core)
+        self.xp = lax.rem(self.d + 2, DP)
+        self.diag = lax.rem(self.sib + 2, DP)
+        self.z = self.s // 2
+        self.y = lax.rem(self.s, 2)
+        self.dp_peers = [self.xp, self.diag, self.sib]
+        self.seq_peers = [lax.rem(self.s + k, SQ) for k in range(1, SQ)]
+        self.yp = (self.d, 2 * self.z + (1 - self.y))
+        self.zp = [lax.rem(self.z + k, ZS) for k in range(1, ZS)]
+        self.zdev = [(self.d, 2 * p + self.y) for p in self.zp]
+
+    def enter(self):
+        peers = [(p, self.s) for p in self.dp_peers] + [(self.d, p) for p in self.seq_peers]
+        bar = pltpu.get_barrier_semaphore()
+        for p in peers:
+            pl.semaphore_signal(bar, inc=1, device_id=p, device_id_type=MESH)
+        pl.semaphore_wait(bar, len(peers))
+
+    def describe(self, i, src, dst, to, j=None):
+        return pltpu.make_async_remote_copy(
+            src_ref=src,
+            dst_ref=dst,
+            send_sem=self.send.at[i],
+            recv_sem=self.recv.at[i if j is None else j],
+            device_id=to,
+            device_id_type=MESH,
+        )
+
+    def local(self, src, dst):
+        c = pltpu.make_async_copy(src, dst, self.lsem.at[self.locals_used])
+        self.locals_used += 1
+        c.start()
+        return c
+
+    def copy(self, src, dst, to, slow=False):
+        c = self.describe(self.used, src, dst, to)
+        self.used += 1
+        c.start()
+        (self.slow if slow else self.sent).append(c)
+        return c
+
+    def settle(self):
+        for c in self.sent:
+            c.wait_send()
+        self.sent = []
+
+    def settle_slow(self):
+        for c in self.slow:
+            c.wait_send()
+        self.slow = []
+
+
+def span(i, rows):
+    return pl.ds(pl.multiple_of(i * rows, 16), rows)
+
+
+def normalize(res):
+    cen = res - jnp.mean(res, axis=-1, keepdims=True)
+    rstd = lax.rsqrt(jnp.mean(cen * cen, axis=-1, keepdims=True) + 1e-05)
+    return cen * rstd, rstd
+
+
+def normalize_back(grad, gain, xhat, rstd):
+    dn = grad * gain
+    return (dn - jnp.mean(dn, axis=-1, keepdims=True) - xhat * jnp.mean(dn * xhat, axis=-1, keepdims=True)) * rstd
+
+
+def pack_pairs(src, dst):
+    half = dst.shape[-1]
+    one, two = pl.ds(0, half), pl.ds(half, half)
+    keep = low_lanes((TOK, half))
+    for e in range(DP):
+        dst[e] = src[pl.ds(ROWS * e, TOK), one]
+        dst[4, pl.ds(PART * e, PART)] = src[pl.ds(ROWS * e + TOK, PART), one]
+        dst[7, pl.ds(PART * e, PART)] = src[pl.ds(ROWS * e + TOK, PART), two]
+    for p in range(2):
+        a = src[pl.ds(ROWS * 2 * p, TOK), two].astype(F32)
+        b = src[pl.ds(ROWS * (2 * p + 1), TOK), two].astype(F32)
+        dst[5 + p] = jnp.where(keep, a, b).astype(BF16)
+
+
+def unpack_pairs(src, dst):
+    half = src.shape[-1]
+    one, two = pl.ds(0, half), pl.ds(half, half)
+    keep = low_lanes((TOK, half))
+    third = [src[5].astype(F32), src[6].astype(F32)]
+    last = jnp.where(keep, src[7].astype(F32), 0.0).astype(BF16)
+    for e in range(DP):
+        dst[pl.ds(ROWS * e, TOK), one] = src[e]
+        mine = third[e // 2]
+        mine = jnp.where(keep, mine, 0.0) if e % 2 == 0 else jnp.where(keep, 0.0, mine)
+        dst[pl.ds(ROWS * e, TOK), two] = mine.astype(BF16)
+        dst[pl.ds(ROWS * e + TOK, PART), one] = src[4, pl.ds(PART * e, PART)]
+        dst[pl.ds(ROWS * e + TOK, PART), two] = last[PART * e : PART * (e + 1)]
+
+
+class Sums:
+    def __init__(self, L, plan, g, ab, f, bufs):
+        self.L, self.plan, self.g, self.ab, self.f, self.bufs = L, plan, g, ab, f, bufs
+        self.end = L.z // 2
+        self.outer = lax.rem(L.z, ZS - 1) == 0
+        self.inner = lax.rem(L.z, ZS - 1) != 0
+        self.inward = (L.d, 2 * (1 + self.end) + L.y)
+        self.outward = (L.d, 2 * (3 * self.end) + L.y)
+        self.across = (L.d, 2 * (3 - L.z) + L.y)
+        self.outer_sent, self.inner_sent, self.todo = [], [], {}
+
+    def send(self, role, i, j, src, dst, to):
+        def make():
+            return self.L.describe(i, src(), dst(), to, j)
+
+        make().start()
+        role.append(make)
+
+    def send_all(self, i, src, dst, to):
+        c = self.L.describe(i, src, dst, to)
+        c.start()
+        self.L.slow.append(c)
+
+    def got(self, i, ref):
+        self.L.describe(i, ref, ref, self.L.yp).wait_recv()
+
+    def start(self, name):
+        kind = self.plan[name][4]
+        self.todo[name] = (self.direct_steps if kind == "d" else self.chain_steps)(name)
+        next(self.todo[name])
+
+    def advance(self, name):
+        next(self.todo[name], None)
+
+    def add(self, where, more):
+        self.g[where] = (self.g[where].astype(F32) + more[...].astype(F32)).astype(BF16)
+
+    def prepare(self, name):
+        at, n, off, width, kind, k0 = self.plan[name][:6]
+        i, l = self.L.used, self.L.locals_used
+        self.L.used += 11
+        self.L.locals_used += 1
+        rows = lambda e: pl.ds(pl.multiple_of(e * HR, HR), HR)
+        cols = lambda e: pl.ds(pl.multiple_of(e * YC + off, 128), width)
+        return i, l, at, pl.ds(at, n), pl.ds(k0, n), rows, cols
+
+    def chain_steps(self, name):
+        L, g, f = self.L, self.g, self.f
+        i, l, at, r, b, rows, cols = self.prepare(name)
+        end, y = self.end, L.y
+        k0 = self.plan[name][5]
+        zfirst = self.plan[name][4] == "z"
+        off, width = self.plan[name][2:4]
+        within = pl.ds(off, width)
+        half = self.bufs.rh.at[b, :, within] if zfirst else None
+        ab = self.ab
+        if zfirst:
+            piece = lambda e: (r, slice(None), cols(e))
+            first, second = self.bufs.zf.at[b, :, within], self.bufs.zs.at[b, :, within]
+            spare = self.bufs.zf
+            final = (r, rows(y), cols(end))
+        else:
+            piece = lambda e: (r, rows(e), cols(y))
+            first, second = self.bufs.pf.at[b, :, within], self.bufs.ps.at[b, :, within]
+            spare = self.bufs.pf
+            ry = self.bufs.ry.at[b, :, within]
+            final = (r, rows(end), cols(y))
+
+        def across_dp(k):
+            p = L.dp_peers[k]
+            return L.describe(i + 3 + k, spare.at[k0 + p, pl.ds(0, HR), within], ab.at[at + L.d, :, within], (p, L.s))
+
+        local = lambda: pltpu.make_async_copy(ab.at[r, :, within], f.at[final], L.lsem.at[l])
+
+        if not zfirst:
+            self.send_all(i, g.at[r, :, cols(1 - y)], ry, L.yp)
+            yield
+            self.got(i, ry)
+            self.add((r, slice(None), cols(y)), ry)
+
+        @pl.when(self.outer)
+        def _():
+            self.send(self.outer_sent, i + 1, i + 1, lambda: g.at[piece(1 - end)], lambda: first, self.inward)
+
+        yield
+
+        @pl.when(self.inner)
+        def _():
+            self.got(i + 1, first)
+            self.add(piece(1 - end), first)
+            self.send(self.inner_sent, i + 1, i + 2, lambda: g.at[piece(1 - end)], lambda: second, self.across)
+
+        yield
+
+        @pl.when(self.inner)
+        def _():
+            self.got(i + 2, second)
+            self.add(piece(end), second)
+            self.send(self.inner_sent, i + 2, i + 2, lambda: g.at[piece(end)], lambda: second, self.outward)
+
+        yield
+        if zfirst:
+
+            @pl.when(self.outer)
+            def _():
+                self.got(i + 2, second)
+                self.add(piece(end), second)
+                self.send(self.outer_sent, i, i, lambda: g.at[r, rows(1 - y), cols(end)], lambda: half, L.yp)
+
+            yield
+
+        @pl.when(self.outer)
+        def _():
+            if zfirst:
+                self.got(i, half)
+                total = g[final].astype(F32) + half[...].astype(F32)
+            else:
+                self.got(i + 2, second)
+                total = g[final].astype(F32) + second[...].astype(F32)
+            if at < 12:
+                spare[b, pl.ds(0, HR), within] = total.astype(BF16)
+                for k in range(DP - 1):
+                    across_dp(k).start()
+                ab[at + L.d, :, within] = spare[k0 + L.d, pl.ds(0, HR), within]
+            else:
+                ab[r, :, within] = total.astype(BF16)
+
+        yield
+
+        @pl.when(self.outer)
+        def _():
+            if at < 12:
+                for k in range(DP - 1):
+                    across_dp(k).wait()
+            self.send(self.outer_sent, i + 6, i + 6, lambda: ab.at[r, :, within], lambda: f.at[final], L.yp if zfirst else self.inward)
+            local().start()
+
+        yield
+        if zfirst:
+
+            @pl.when(self.outer)
+            def _():
+                self.got(i + 6, ab.at[r, :, within])
+                local().wait()
+                self.send(self.outer_sent, i + 9, i + 9, lambda: f.at[piece(end)], lambda: f.at[piece(end)], self.inward)
+
+            yield
+
+        @pl.when(self.inner)
+        def _():
+            self.got(i + (9 if zfirst else 6), f.at[piece(end)])
+            self.send(self.inner_sent, i + 7, i + 7, lambda: f.at[piece(end)], lambda: f.at[piece(end)], self.across)
+
+        yield
+
+        @pl.when(self.inner)
+        def _():
+            self.got(i + 7, f.at[piece(1 - end)])
+            self.send(self.inner_sent, i + 8, i + 8, lambda: f.at[piece(1 - end)], lambda: f.at[piece(1 - end)], self.outward)
+
+        yield
+
+        @pl.when(self.outer)
+        def _():
+            self.got(i + 8, f.at[piece(1 - end)])
+            if not zfirst:
+                local().wait()
+
+        if not zfirst:
+            whole = f.at[r, :, cols(y)]
+            self.send_all(i + 9, whole, whole, L.yp)
+            yield
+            self.got(i + 9, whole)
+
+    def direct_steps(self, name):
+        L, g, f = self.L, self.g, self.f
+        i, l, at, r, b, rows, cols = self.prepare(name)
+        n, off, width = self.plan[name][1:4]
+        mine = cols(L.y)
+        within = pl.ds(off, width)
+        ry = self.bufs.ry.at[b, :, within]
+        quarter = lambda z: pl.ds(pl.multiple_of(z * (HR // 2), HR // 2), HR // 2)
+        own = (r, quarter(L.z), mine)
+        k1 = self.plan[name][6]
+        c = pl.ds(k1, n)
+        got, out, ab = self.bufs.qz, self.bufs.qo, self.bufs.qa
+        self.send_all(i, g.at[r, :, cols(1 - L.y)], ry, L.yp)
+        yield
+        self.got(i, ry)
+        self.add((r, slice(None), mine), ry)
+        for k in range(ZS - 1):
+            self.send_all(i + 1 + k, g.at[r, quarter(L.zp[k]), mine], got.at[k, c, :, within], L.zdev[k])
+        yield
+        total = g[own].astype(F32)
+        for k in range(ZS - 1):
+            self.got(i + 1 + k, got.at[k, c, :, within])
+            total = total + got[k, c, :, within].astype(F32)
+        if at < 12:
+            out[c, :, within] = total.astype(BF16)
+            for k, p in enumerate(L.dp_peers):
+                self.send_all(i + 4 + k, out.at[k1 + p, :, within], ab.at[k1 + L.d, :, within], (p, L.s))
+            ab[k1 + L.d, :, within] = out[k1 + L.d, :, within]
+            yield
+            for k in range(DP - 1):
+                self.got(i + 4 + k, ab.at[k1, :, within])
+        else:
+            ab[c, :, within] = total.astype(BF16)
+        local = pltpu.make_async_copy(ab.at[c, :, within], f.at[own], L.lsem.at[l])
+        local.start()
+        for k in range(ZS - 1):
+            self.send_all(i + 7 + k, ab.at[c, :, within], f.at[own], L.zdev[k])
+        yield
+        local.wait()
+        for k in range(ZS - 1):
+            self.got(i + 7 + k, f.at[own])
+        whole = f.at[r, :, mine]
+        self.send_all(i + 10, whole, whole, L.yp)
+        yield
+        self.got(i + 10, whole)
+
+    def settle(self):
+        @pl.when(self.outer)
+        def _():
+            for make in self.outer_sent:
+                make().wait_send()
+
+        @pl.when(self.inner)
+        def _():
+            for make in self.inner_sent:
+                make().wait_send()
+
+
+class Stage:
+    def __init__(self, buf, sem):
+        self.buf, self.sem, self.count, self.open = buf, sem, 0, {}
+
+    def slot(self):
+        i = self.count % STAGES
+        if i in self.open:
+            self.open.pop(i).wait()
+        return self.buf.at[i]
+
+    def go(self, dst):
+        i = self.count % STAGES
+        c = pltpu.make_async_copy(self.buf.at[i], dst, self.sem.at[i])
+        c.start()
+        self.open[i] = c
+        self.count += 1
+
+    def settle(self):
+        for c in self.open.values():
+            c.wait()
+
+
+def widen_kernel(f0, f1, rows_out, rows_in, *refs):
+    outs, (o_out, o_in, buf, stage_buf, in_sem, out_sem) = refs[:10], refs[10:]
+    stage = Stage(stage_buf, out_sem)
+    moves = [
+        pltpu.make_async_copy(rows_out, o_out, in_sem.at[10]),
+        pltpu.make_async_copy(rows_in, o_in, in_sem.at[11]),
+    ]
+    for c in moves:
+        c.start()
+    keep = low_lanes((QR, 128))
+    loads = {}
+    for l, f in ((0, f0), (1, f1)):
+        for k, (at, n) in enumerate(CHUNKS.values()):
+            c = pltpu.make_async_copy(f.at[pl.ds(at, n)], buf.at[l, pl.ds(at, n)], in_sem.at[5 * l + k])
+            c.start()
+            loads[5 * l + k] = c
+    for l in range(2):
+        o_qkv, o_out, o_gate, o_up, o_down = outs[5 * l : 5 * l + 5]
+        g = buf.at[l]
+        for k, (name, (at, n)) in enumerate(CHUNKS.items()):
+            loads[5 * l + k].wait()
+            for i in range(3 if name == "qkv" else n):
+                st = stage.slot()
+                if name == "qkv":
+                    one, two = pl.ds(128 * i, 128), pl.ds(384 + 128 * i, 128)
+                    for a in range(2):
+                        po = flip(g[2 * a + 1, :, one].astype(F32))
+                        te, to = g[2 * a, :, two].astype(F32), g[2 * a + 1, :, two].astype(F32)
+                        st[:, pl.ds(384 * a, 128)] = g[2 * a, :, one].astype(F32)
+                        st[:, pl.ds(384 * a + 128, 128)] = jnp.where(keep, te + flip(te), po)
+                        st[:, pl.ds(384 * a + 256, 128)] = jnp.where(keep, po, to + flip(to))
+                    dst = o_qkv.at[:, pl.ds(D * i, D)]
+                else:
+                    st[...] = g[at + i].astype(F32)
+                    if name == "out":
+                        dst = o_out
+                    elif name == "down":
+                        dst = o_down.at[pl.ds(QR * i, QR)]
+                    else:
+                        dst = (o_gate if name == "gate" else o_up).at[:, pl.ds(D * i, D)]
+                stage.go(dst)
+    stage.settle()
+    for c in moves:
+        c.wait()
+
+
+CHUNKS = {"qkv": (0, 4), "gate": (4, 4), "up": (8, 4), "down": (12, 4), "out": (16, 1)}
+BLOCKS = 17
+ZS = 4
+QR = D // DP
+HR = QR // 2
+YC = D // 2
+PLAN = [
+    {
+        "d": (12, 4, 0, 256, "y", 0, 0),
+        "D": (12, 4, 256, 128, "y", 0, 0),
+        "g": (4, 4, 0, 256, "z", 0, 0),
+        "G": (4, 4, 256, 128, "z", 0, 0),
+        "u": (8, 4, 0, 256, "y", 4, 0),
+        "U": (8, 4, 256, 128, "y", 4, 0),
+        "o": (16, 1, 0, YC, "y", 8, 0),
+        "q": (0, 4, 0, 256, "d", 9, 0),
+        "r": (0, 4, 256, 128, "d", 9, 0),
+    },
+    {
+        "d": (12, 4, 0, 256, "d", 12, 12),
+        "D": (12, 4, 256, 128, "d", 12, 12),
+        "g": (4, 4, 0, 256, "d", 4, 4),
+        "G": (4, 4, 256, 128, "d", 4, 4),
+        "u": (8, 4, 0, 256, "d", 8, 8),
+        "U": (8, 4, 256, 128, "d", 8, 8),
+        "o": (16, 1, 0, YC, "d", 16, 16),
+        "q": (0, 4, 0, 256, "d", 0, 0),
+        "r": (0, 4, 256, 128, "d", 0, 0),
+    },
+]
+STAGES = 8
+SEMS = 480
+
+INS = ["inp", "cot", "aux", "wq0", "wg0", "wu0", "wo0", "wd0", "wq1", "wg1", "wu1", "wo1", "wd1", "cosf", "sinf"]
+INS_ANY = {"wq0", "wg0", "wu0", "wd0", "wq1", "wg1", "wu1", "wd1"}
+GRADS = [((QR, 3 * D), F32), ((QR, D), F32), ((QR, DP * D), F32), ((QR, DP * D), F32), ((D, D), F32)]
+BIG = ((ALL, D), BF16)
+OUTS = [("out", ((2, TOK, D), BF16)), ("gin", ((2, TOK, D), BF16)), ("vsum", ((8, D), F32))]
+OUTS_ANY = [("fs" + str(i), ((BLOCKS, QR, D), BF16)) for i in range(2)] + [("st" + str(i), BIG) for i in range(5)] + [("sx0", ((ROWS, D), F32)), ("sx1", ((ROWS, D), F32)), ("sx2", ((LEN, 128), F32))]
+TALL = ((LEN, 128), BF16)
+SCRATCH = (
+    [
+        (n + str(l), s)
+        for l in range(2)
+        for n, s in [
+            ("qkv", ((LEN, 384), BF16)),
+            ("lse", ((8, LEN), F32)),
+            ("ce", ((ALL, 256), BF16)),
+            ("ra", ((ROWS, 128), F32)),
+            ("rf", ((ROWS, 128), F32)),
+            ("wqg", ((D, D), BF16)),
+            ("wgg", ((D, D), BF16)),
+            ("wug", ((D, D), BF16)),
+            ("wog", ((256, D), BF16)),
+            ("g", ((BLOCKS, QR, D), BF16)),
+            ("ry", ((13 + 4 * l, QR, YC), BF16)),
+            ("qz", ((ZS - 1, 4 + 13 * l, HR // 2, YC), BF16)),
+            ("qo", ((4 + 13 * l, HR // 2, YC), BF16)),
+            ("qa", ((4 + 13 * l, HR // 2, YC), BF16)),
+        ]
+    ]
+    + [
+        ("x", BIG),
+        ("wd", ((D, D), BF16)),
+        ("xa", ((ROWS, D), F32)),
+        ("xf", ((ROWS, D), F32)),
+        ("ctx", ((LEN, 128), F32)),
+        ("actf", BIG),
+        ("gp", BIG),
+        ("up", BIG),
+        ("hid", BIG),
+        ("part", ((ALL, D), F32)),
+        ("ta", BIG),
+        ("tb", BIG),
+        ("db", BIG),
+        ("dsb", BIG),
+        ("sb", ((SQ, TOK, 384), BF16)),
+        ("sc", ((SQ, TOK, 128), BF16)),
+        ("rx", ((SQ, TOK, 384), BF16)),
+        ("rc", ((SQ, TOK, 128), BF16)),
+        ("dc", TALL),
+        ("cb", TALL),
+        ("kz", ((2, LEN, 128), BF16)),
+        ("vz", ((2, LEN, 128), BF16)),
+        ("kt", ((2, 128, LEN), BF16)),
+        ("et", ((128, LEN), F32)),
+        ("cz", ((2, LEN, 128), BF16)),
+        ("inner", ((8, LEN), F32)),
+        ("hres", ((ROWS, D), F32)),
+        ("gres", ((ROWS, D), F32)),
+        ("nv", ((8, D), F32)),
+        ("auxs", ((DP, 16, 256), F32)),
+        ("cbuf", ((DP, 2, PART, D), BF16)),
+        ("loa", ((2, DP, PART, D), BF16)),
+        ("los", ((2, PART, D), BF16)),
+        ("ab", ((BLOCKS, HR, YC), BF16)),
+        ("rh", ((4, HR, YC), BF16)),
+        ("pf", ((9, HR, YC), BF16)),
+        ("ps", ((9, HR, YC), BF16)),
+        ("zf", ((4, QR, YC), BF16)),
+        ("zs", ((4, QR, YC), BF16)),
+        ("va", ((8, D), F32)),
+        ("vb", ((8, D), F32)),
+        ("vc", ((8, D), F32)),
+        ("vd", ((8, D), F32)),
+        ("vy", ((8, D), F32)),
+        ("vz3", ((ZS - 1, 8, D), F32)),
+        ("vs", ((8, D), F32)),
+        ("vx", ((8, D), F32)),
+    ]
+    + [(n + k, s) for k in "af" for n, s in [("snd", ((2, ROWS, D), BF16)), ("got", ((2, ROWS, D), BF16)), ("mid", ((ROWS, D), BF16)), ("fin", ((ROWS, D), BF16))]]
+)
+
+
+class Named:
+    pass
+
+
+def whole_kernel(*refs):
+    R = Named()
+    names = INS + [n for n, _ in OUTS + OUTS_ANY + SCRATCH]
+    for n, r in zip(names, refs):
+        setattr(R, n, r)
+    L = Links(*refs[len(names) :])
+    d, s = L.d, L.s
+    own = pl.ds(pl.multiple_of(d * ROWS, 32), ROWS)
+    tok = pl.ds(pl.multiple_of(s * TOK, TOK), TOK)
+
+    def at_layer(n, l):
+        return getattr(R, n + str(l))
+
+    def chip(c):
+        return pl.ds(pl.multiple_of(c * HALF, 32), HALF)
+
+    local = L.local
+
+    def rows_at(ref, i):
+        return ref.at[span(i, ROWS)]
+
+    def input_at(ref, i):
+        return ref.at[pl.ds(2 * i, 2), pl.ds(0, TOK)]
+
+    def gather_begin(ref, at=rows_at):
+        far = L.copy(at(ref, d), at(ref, d), (L.xp, s))
+        near = L.copy(at(ref, d), at(ref, d), (L.sib, s))
+        return near, far
+
+    def gather_forward(ref, far, at=rows_at):
+        far.wait_recv()
+        return L.copy(at(ref, L.xp), at(ref, L.xp), (L.sib, s))
+
+    part = R.part
+
+    def reduce_chip(k, i):
+        snd, got = getattr(R, "snd" + k), getattr(R, "got" + k)
+        snd[i] = part[span(L.diag if i else L.sib, ROWS)].astype(BF16)
+        return L.copy(snd.at[i], got.at[i], (L.sib, s))
+
+    def reduce_cross(k, c_other):
+        got, mid, fin = getattr(R, "got" + k), getattr(R, "mid" + k), getattr(R, "fin" + k)
+        c_other.wait_recv()
+        mid[...] = (part[span(L.xp, ROWS)] + got[1].astype(F32)).astype(BF16)
+        return L.copy(mid, fin, (L.xp, s))
+
+    def reduce_end(k, c_own, c_cross):
+        got, fin = getattr(R, "got" + k), getattr(R, "fin" + k)
+        c_own.wait_recv()
+        c_cross.wait_recv()
+        return part[own] + got[0].astype(F32) + fin[...].astype(F32)
+
+    lqs = [
+        [local(getattr(R, "wq" + str(l)).at[:, pl.ds(D * t, D)], R.g1.at[8 + 3 * l + t]) for t in range(3)]
+        for l in range(2)
+    ]
+    mycols = pl.ds(pl.multiple_of(d * D, D), D)
+    mydep = pl.ds(pl.multiple_of(d * QR, 64), QR)
+    lws = []
+    for l in range(2):
+        for n in "gu":
+            lws.append(local(getattr(R, "w" + n + str(l)).at[:, mycols], at_layer("w" + n + "g", l).at[mydep]))
+    lws.append(local(R.wd0, R.wd))
+    inb = R.g0
+    inb[pl.ds(2 * d, 2), pl.ds(0, TOK)] = R.inp[...]
+    R.auxs[d] = R.aux[...]
+    L.enter()
+    small = [L.copy(R.aux, R.auxs.at[d], (p, s)) for p in L.dp_peers]
+
+    hq = QR // 2
+    mine_half = L.y * hq
+
+    def arrange_qkv(l):
+        for c in lqs[l]:
+            c.wait()
+        keep = low_lanes((QR, 128))
+        for t in range(3):
+            for a in range(2):
+                t0, t1, t2 = [R.g1[8 + 3 * l + t, :, pl.ds(384 * a + 128 * i, 128)].astype(F32) for i in range(3)]
+                f1, f2 = flip(t1), flip(t2)
+                for p, one, two in (
+                    (2 * a, t0, jnp.where(keep, t1, f1)),
+                    (2 * a + 1, jnp.where(keep, f1, f2), jnp.where(keep, f2, t2)),
+                ):
+                    R.g1[4 * l + p, :, pl.ds(128 * t, 128)] = one.astype(BF16)
+                    R.g1[4 * l + p, :, pl.ds(384 + 128 * t, 128)] = two.astype(BF16)
+
+    def share_qkv(l):
+        w = at_layer("wqg", l)
+        far = []
+        for p in (L.xp, L.diag):
+            src = R.g1.at[4 * l + p, pl.ds(pl.multiple_of(mine_half, 32), hq)]
+            far.append(L.copy(src, w.at[pl.ds(pl.multiple_of(d * QR + mine_half, 32), hq)], (p, s), True))
+        near = L.copy(R.g1.at[4 * l + L.sib], w.at[mydep], (L.sib, s), True)
+        w[mydep] = R.g1[4 * l + d]
+        return [(w, far, near)]
+
+    def share_ff(l):
+        res = []
+        for n in "gu":
+            w, g = getattr(R, "w" + n + str(l)), at_layer("w" + n + "g", l)
+            far = []
+            half = pl.ds(pl.multiple_of(mine_half, 32), hq)
+            for p in (L.xp, L.diag):
+                src = w.at[half, pl.ds(pl.multiple_of(p * D, D), D)]
+                far.append(L.copy(src, g.at[pl.ds(pl.multiple_of(d * QR + mine_half, 32), hq)], (p, s), True))
+            near = L.copy(w.at[:, pl.ds(pl.multiple_of(L.sib * D, D), D)], g.at[mydep], (L.sib, s), True)
+            res.append((g, far, near))
+        return res
+
+    def pass_on(shares):
+        res = []
+        for w, far, near in shares:
+            for c, p in zip(far, (L.xp, L.diag)):
+                c.wait_recv()
+                o = pl.ds(pl.multiple_of(p * QR + mine_half, 32), hq)
+                res.append(L.copy(w.at[o], w.at[o], L.yp, True))
+            res.append(near)
+        return res
+
+    arrange_qkv(0)
+    sq = share_qkv(0)
+    near, far = gather_begin(inb, input_at)
+    for l in range(2):
+        wo, wog = getattr(R, "wo" + str(l)), at_layer("wog", l)
+        wog[pl.ds(0, QR)] = wo[...]
+        wog[pl.ds(QR, 64)] = wo[pl.ds(128, 64)]
+    arrange_qkv(1)
+    for c in small:
+        c.wait_recv()
+    keep8 = low_lanes((8, 128))
+    for a in range(2):
+        e, o = R.auxs.at[2 * a], R.auxs.at[2 * a + 1]
+        eight = pl.ds(0, 8)
+        lo, hi = pl.ds(0, 128), pl.ds(128, 128)
+        po = flip(o[eight, lo])
+        R.nv[:, pl.ds(384 * a, 128)] = e[eight, lo]
+        R.nv[:, pl.ds(384 * a + 128, 128)] = jnp.where(keep8, e[eight, hi], po)
+        R.nv[:, pl.ds(384 * a + 256, 128)] = jnp.where(keep8, po, flip(o[eight, hi]))
+
+    def flag(j, m):
+        v = R.auxs[j, 8 + m : 9 + m]
+        return jnp.concatenate([v, v, v], axis=1)
+
+    f0 = flag(0, 0) * flag(1, 0) * flag(2, 0) * flag(3, 0)
+    f1 = 1.0 - f0
+    lone_flag = [f0 * flag(j, 1) + f1 * flag(j, 0) for j in range(DP)]
+    lone_mine = f0 * flag(d, 1) + f1 * flag(d, 0)
+
+    shares = pass_on(sq)
+    fwd = gather_forward(inb, far, input_at)
+    near.wait_recv()
+    fwd.wait_recv()
+    lone = None
+    for j in range(DP):
+        a = inb[2 * j, pl.ds(0, TOK)].astype(F32)
+        b = inb[2 * j + 1, pl.ds(0, TOK)].astype(F32)
+        R.x[pl.ds(ROWS * j, TOK)] = (f0 * a + f1 * b).astype(BF16)
+        term = lone_flag[j] * (f0 * b + f1 * a)
+        lone = term if lone is None else lone + term
+    lone = lone.astype(BF16)
+    for j in range(DP):
+        R.x[pl.ds(ROWS * j + TOK, PART)] = lone[PART * j : PART * (j + 1)]
+    R.hres[...] = R.x[own].astype(F32)
+    for c in shares:
+        c.wait_recv()
+
+    later = {}
+    stash = []
+
+    def forward(l):
+        x = R.x
+        ctx = R.ctx
+        qkv, lse, ce = [at_layer(n, l) for n in ("qkv", "lse", "ce")]
+        wq, wg, wu, wo = [at_layer(n, l) for n in ("wqg", "wgg", "wug", "wog")]
+        wd = R.wd
+        qx = R.ta
+
+        def project(c):
+            rows = chip(c)
+            a = x[rows]
+            y = [mm(a, wq[:, pl.ds(256 * t, 256)]) for t in range(3)]
+            for b in range(2):
+                j = 2 * c + b
+                lone_at = pl.ds(pl.multiple_of(s * TOK + j * PART, PART), PART)
+                co = jnp.concatenate([R.cosf[tok], R.cosf[lone_at]], axis=0)
+                si = jnp.concatenate([R.sinf[tok], R.sinf[lone_at]], axis=0)
+                for t in range(6):
+                    v = y[t // 2][ROWS * b : ROWS * (b + 1), 128 * (t % 2) : 128 * (t % 2 + 1)]
+                    if t % 3 != 2:
+                        v = v * co + swap_halves(v) * si
+                    if t % 3 == 0:
+                        v = v * (HEAD**-0.5)
+                    qx[span(j, ROWS), pl.ds(128 * t, 128)] = v.astype(BF16)
+
+        if l == 0:
+            project(0)
+            project(1)
+            keep_x = local(x, R.st4)
+        else:
+            x[own] = R.hres[...].astype(BF16)
+            near, far = gather_begin(x)
+            near.wait_recv()
+            project(L.x)
+            fwd = gather_forward(x, far)
+            fwd.wait_recv()
+            project(1 - L.x)
+
+        for c in stash:
+            c.wait()
+        del stash[:]
+        pack_pairs(qx, R.sb)
+        qkv[tok] = R.sb[s]
+        qc = [L.copy(R.sb.at[p], qkv.at[tok], (d, p)) for p in L.seq_peers]
+        cc = []
+        ff = share_ff(l)
+        if l == 0:
+            for p in L.dp_peers:
+                r = pl.ds(pl.multiple_of(p * PART, PART), PART)
+                cc.append(L.copy(R.cot.at[:, r, :], R.cbuf.at[d], (p, s)))
+            R.cbuf[d] = R.cot[:, pl.ds(pl.multiple_of(d * PART, PART), PART), :]
+        for c in qc:
+            c.wait_recv()
+
+        keep = low_lanes((LEN, 128))
+        k = qkv[:, pl.ds(128, 128)].astype(F32)
+        R.kz[0] = jnp.where(keep, k, 0.0).astype(BF16)
+        R.kz[1] = jnp.where(keep, 0.0, k).astype(BF16)
+        base = L.used
+        L.used += SQ
+
+        def back(p, i):
+            r = pl.ds(pl.multiple_of(p * TOK, TOK), TOK)
+            return L.describe(i, R.cb.at[r], R.rc.at[s], (d, p))
+
+        @pl.loop(0, LEN // QB)
+        def _(i):
+            at = pl.ds(pl.multiple_of(i * QB, QB), QB)
+            q = qkv[at, pl.ds(0, 128)]
+            outs, logs = [], []
+            for j in range(2):
+                sc = mm_t(q, R.kz[j])
+                top = jnp.max(sc, axis=-1, keepdims=True)
+                ex = jnp.exp(sc - top)
+                tot = jnp.sum(ex, axis=-1, keepdims=True)
+                o = mm(ex.astype(BF16), qkv[:, pl.ds(256, 128)])
+                outs.append(o / tot)
+                logs.append(jnp.broadcast_to(top + jnp.log(tot), (QB, 128)))
+            pick = low_lanes((QB, 128))
+            c = jnp.where(pick, outs[0], outs[1])
+            ctx[at] = c
+            R.et[:, at] = jnp.where(pick, logs[0], logs[1]).T
+            R.cb[at] = c.astype(BF16)
+            for h in range(QB // TOK):
+                p = (QB // TOK) * i + h
+                k = lax.rem(p - s + SQ, SQ)
+
+                @pl.when(k != 0)
+                def _():
+                    back(p, base + k).start()
+
+        lse[0:1] = R.et[0:1]
+        lse[1:2] = R.et[64:65]
+        R.rc[s] = R.cb[tok]
+        ffp = pass_on(ff)
+        if l == 0:
+            later["q"] = share_qkv(1)
+            for c in cc:
+                c.wait_recv()
+            a = R.cot[0].astype(F32)
+            b = R.cot[1].astype(F32)
+            R.gres[pl.ds(0, TOK)] = f0 * a + f1 * b
+            lone = None
+            for j in range(DP):
+                term = lone_flag[j] * (f0 * R.cbuf[j, 1].astype(F32) + f1 * R.cbuf[j, 0].astype(F32))
+                lone = term if lone is None else lone + term
+            R.gres[pl.ds(TOK, PART)] = lone
+        for k in range(1, SQ):
+            back(L.seq_peers[k - 1], base + k).wait_recv()
+        unpack_pairs(R.rc, ce)
+
+        for c in (1 - L.x, L.x):
+            a = ce[chip(c)]
+            for t in range(3):
+                cs = pl.ds(256 * t, 256)
+                part[chip(c), cs] = mm(a, wo[:, cs])
+        for k in range(1, SQ):
+            back(L.seq_peers[k - 1], base + k).wait_send()
+        L.settle()
+        if l == 0:
+            keep_x.wait()
+        c_other = reduce_chip("a", 1)
+        c_own = reduce_chip("a", 0)
+        c_cross = reduce_cross("a", c_other)
+        res = R.hres[...] + reduce_end("a", c_own, c_cross)
+        n = 4 * l
+        xhat, rstd = normalize(res)
+        norm_a = xhat * R.nv[n : n + 1] + R.nv[n + 1 : n + 2]
+        R.actf[own] = norm_a.astype(BF16)
+        near, far = gather_begin(R.actf)
+        R.hres[...] = norm_a
+        R.xa[...] = xhat
+        at_layer("ra", l)[...] = jnp.broadcast_to(rstd, (ROWS, 128))
+        if l == 0:
+            for c in lws:
+                c.wait()
+        for c in ffp:
+            c.wait_recv()
+
+        def feed(rows):
+            a = R.actf[rows]
+            for t in range(3):
+                cs = pl.ds(256 * t, 256)
+                gp = mm(a, wg[:, cs])
+                up = mm(a, wu[:, cs])
+                R.gp[rows, cs] = gp.astype(BF16)
+                R.up[rows, cs] = up.astype(BF16)
+                R.hid[rows, cs] = (gp * jax.nn.sigmoid(gp) * up).astype(BF16)
+            h = R.hid[rows]
+            for t in range(3):
+                cs = pl.ds(256 * t, 256)
+                part[rows, cs] = mm(h, wd[:, cs])
+
+        near.wait_recv()
+        feed(chip(L.x))
+        L.settle()
+        c_own = reduce_chip("f", 0)
+        fwd = gather_forward(R.actf, far)
+        fwd.wait_recv()
+        feed(chip(1 - L.x))
+        c_other = reduce_chip("f", 1)
+        c_cross = reduce_cross("f", c_other)
+        if l == 0:
+            later["q"] = pass_on(later["q"])
+            for i, r in enumerate((R.actf, R.gp, R.up, R.hid)):
+                stash.append(local(r, getattr(R, "st" + str(i))))
+            stash.append(local(R.xa, R.sx0))
+            stash.append(local(R.ctx, R.sx2))
+            stash.append(local(R.wd1, R.wd))
+            for c in later["q"]:
+                c.wait_recv()
+        res = R.hres[...] + reduce_end("f", c_own, c_cross)
+        xhat, rstd = normalize(res)
+        h = xhat * R.nv[n + 2 : n + 3] + R.nv[n + 3 : n + 4]
+        R.xf[...] = xhat
+        if l == 0:
+            stash.append(local(R.xf, R.sx1))
+        at_layer("rf", l)[...] = jnp.broadcast_to(rstd, (ROWS, 128))
+        R.hres[...] = h
+        L.settle()
+
+    def lone_begin(k, rows):
+        R.los[k] = rows.astype(BF16)
+        R.loa[k, d] = rows.astype(BF16)
+        return [L.copy(R.los.at[k], R.loa.at[k, d], (p, s)) for p in L.dp_peers]
+
+    def lone_end(k, copies, whole, dst):
+        for c in copies:
+            c.wait_recv()
+        lone = lone_mine * R.loa[k].reshape(TOK, D).astype(F32)
+        dst[0] = (f0 * whole + f1 * lone).astype(BF16)
+        dst[1] = (f1 * whole + f0 * lone).astype(BF16)
+
+    forward(0)
+    forward(1)
+    lone_out = lone_begin(0, R.hres[pl.ds(TOK, PART)])
+
+
+    def tick(codes):
+        for c in codes:
+            total = sums[int(c[1])]
+            total.advance(c[0]) if c[0] in total.todo else total.start(c[0])
+
+    sums = []
+    for l in range(2):
+        bufs = Named()
+        for n in ("rh", "pf", "ps", "zf", "zs"):
+            setattr(bufs, n, getattr(R, n))
+        for n in ("ry", "qz", "qo", "qa"):
+            setattr(bufs, n, at_layer(n, l))
+        sums.append(Sums(L, PLAN[l], at_layer("g", l), R.ab, at_layer("fs", l), bufs))
+    R.va[...] = jnp.zeros_like(R.va)
+
+    def backward(l, ticks):
+        x = R.x
+        ctx = R.ctx
+        qkv, lse, ce = [at_layer(n, l) for n in ("qkv", "lse", "ce")]
+        wq, wg, wu, wo = [at_layer(n, l) for n in ("wqg", "wgg", "wug", "wog")]
+        wd = R.wd
+        g, n, total = at_layer("g", l), 4 * l, sums[l]
+
+        def grad_of(name, a, b):
+            at, c = CHUNKS[name]
+            for t in range(3):
+                cs = pl.ds(256 * t, 256)
+                g[pl.ds(at, c), :, cs] = t_mm(a[...], b[:, cs]).astype(BF16).reshape(c, QR, 256)
+            for k in PLAN[l]:
+                if PLAN[l][k][0] == at and k + str(l) not in LATER:
+                    total.start(k)
+
+        grad = R.gres[...]
+        xhat = R.xf[...]
+        d_res_f = normalize_back(grad, R.nv[n + 2 : n + 3], xhat, at_layer("rf", l)[:, 0:1])
+        R.db[own] = d_res_f.astype(BF16)
+        near, far = gather_begin(R.db)
+        R.va[n + 2 : n + 3] = jnp.sum(grad * xhat, axis=0, keepdims=True)
+        R.va[n + 3 : n + 4] = jnp.sum(grad, axis=0, keepdims=True)
+        R.gres[...] = d_res_f
+        tick(ticks.get(0, ()))
+
+        def feed(rows):
+            a = R.db[rows]
+            for t in range(3):
+                cs = pl.ds(256 * t, 256)
+                dh = mm_t(a, wd[cs])
+                gv, uv = R.gp[rows, cs].astype(F32), R.up[rows, cs].astype(F32)
+                sig = jax.nn.sigmoid(gv)
+                R.ta[rows, cs] = (dh * uv * sig * (1.0 + gv * (1.0 - sig))).astype(BF16)
+                R.tb[rows, cs] = (dh * gv * sig).astype(BF16)
+            dgv, duv = R.ta[rows], R.tb[rows]
+            for t in range(3):
+                cs = pl.ds(256 * t, 256)
+                part[rows, cs] = mm_t(dgv, wg[cs]) + mm_t(duv, wu[cs])
+
+        near.wait_recv()
+        feed(chip(L.x))
+        L.settle()
+        c_own = reduce_chip("f", 0)
+        fwd = gather_forward(R.db, far)
+        fwd.wait_recv()
+        feed(chip(1 - L.x))
+        c_other = reduce_chip("f", 1)
+        c_cross = reduce_cross("f", c_other)
+        grad_of("down", R.hid, R.db)
+        grad_of("gate", R.actf, R.ta)
+        grad_of("up", R.actf, R.tb)
+        tick(ticks.get(1, ()))
+        d_norm = R.gres[...] + reduce_end("f", c_own, c_cross)
+        L.settle()
+        xhat = R.xa[...]
+        d_res_a = normalize_back(d_norm, R.nv[n : n + 1], xhat, at_layer("ra", l)[:, 0:1])
+        R.dsb[own] = d_res_a.astype(BF16)
+        near, far = gather_begin(R.dsb)
+        R.va[n : n + 1] = jnp.sum(d_norm * xhat, axis=0, keepdims=True)
+        R.va[n + 1 : n + 2] = jnp.sum(d_norm, axis=0, keepdims=True)
+        R.gres[...] = d_res_a
+        tick(ticks.get(2, ()))
+        reload = []
+        if l == 1:
+            for i, r in enumerate((R.actf, R.gp, R.up, R.hid)):
+                reload.append(local(getattr(R, "st" + str(i)), r))
+            reload.append(local(R.sx0, R.xa))
+            reload.append(local(R.sx1, R.xf))
+            reload.append(local(R.wd0, R.wd))
+        fwd = gather_forward(R.dsb, far)
+        near.wait_recv()
+        fwd.wait_recv()
+        R.ta[:, pl.ds(0, 256)] = mm_t(R.dsb[...], wo[...]).astype(BF16)
+        pack_pairs(R.ta.at[:, pl.ds(0, 256)], R.sc)
+        R.dc[tok] = R.sc[s]
+        qc = [L.copy(R.sc.at[p], R.dc.at[tok], (d, p)) for p in L.seq_peers]
+
+        g_out = t_mm(ce[...], R.dsb[...])
+        o = CHUNKS["out"][0]
+        g[o, pl.ds(0, 128)] = g_out[0:128].astype(BF16)
+        g[o, pl.ds(128, 64)] = (g_out[128:192] + g_out[192:256]).astype(BF16)
+        total.start("o")
+        keep = low_lanes((LEN, 128))
+        k = qkv[:, pl.ds(128, 128)].astype(F32)
+        k0, k1 = jnp.where(keep, k, 0.0), jnp.where(keep, 0.0, k)
+        R.kz[0] = k0.astype(BF16)
+        R.kz[1] = k1.astype(BF16)
+        R.kt[0] = k0.T.astype(BF16)
+        R.kt[1] = k1.T.astype(BF16)
+        q = qkv[:, pl.ds(0, 128)].astype(F32)
+        R.vz[0] = jnp.where(keep, q, 0.0).astype(BF16)
+        R.vz[1] = jnp.where(keep, 0.0, q).astype(BF16)
+        tick(ticks.get(3, ()))
+        for c in qc:
+            c.wait_recv()
+        tick(ticks.get(7, ()))
+        g2 = R.dc[...].astype(F32)
+        et = (g2 * ctx[...]).T
+        R.inner[0:1] = jnp.sum(et[0:64], axis=0, keepdims=True)
+        R.inner[1:2] = jnp.sum(et[64:128], axis=0, keepdims=True)
+        R.cz[0] = jnp.where(keep, g2, 0.0).astype(BF16)
+        R.cz[1] = jnp.where(keep, 0.0, g2).astype(BF16)
+        if l == 1:
+            reload.append(local(R.sx2, ctx))
+        R.et[...] = jnp.zeros_like(R.et)
+        base = L.used
+        L.used += SQ
+
+        def unrotate(v, co, si):
+            return v * co - swap_halves(v) * si
+
+        kv = pl.ds(128, 256)
+
+        def back(p, i):
+            return L.describe(i, R.sb.at[p, :, kv], R.rx.at[s, :, kv], (d, p))
+
+        @pl.loop(0, LEN // QB)
+        def _(i):
+            at = pl.ds(pl.multiple_of(i * QB, QB), QB)
+            v = qkv[at, pl.ds(256, 128)]
+            vf = v.astype(F32)
+            pick = low_lanes((QB, 128))
+            dk, dv = None, None
+            for j in range(2):
+                vz = (jnp.where(pick, vf, 0.0) if j == 0 else jnp.where(pick, 0.0, vf)).astype(BF16)
+                pr = jnp.exp(mm_t(R.kz[j, at], qkv[:, pl.ds(0, 128)]) - lse[pl.ds(j, 1)])
+                dp = mm_t(vz, R.dc[...])
+                ds = (pr * (dp - R.inner[pl.ds(j, 1)])).astype(BF16)
+                a = mm(pr.astype(BF16), R.cz[j])
+                b = mm(ds, R.vz[j])
+                dv = a if dv is None else dv + a
+                dk = b if dk is None else dk + b
+                R.et[...] += mm(R.kt[j, :, at], ds)
+            dk = unrotate(dk, R.cosf[at], R.sinf[at]).astype(BF16)
+            dv = dv.astype(BF16)
+            for h in range(QB // TOK):
+                p = (QB // TOK) * i + h
+                R.sb[p, :, pl.ds(128, 128)] = dk[TOK * h : TOK * (h + 1)]
+                R.sb[p, :, pl.ds(256, 128)] = dv[TOK * h : TOK * (h + 1)]
+                k = lax.rem(p - s + SQ, SQ)
+
+                @pl.when(k != 0)
+                def _():
+                    back(p, base + k).start()
+
+        dq = unrotate(R.et[...].T * (HEAD**-0.5), R.cosf[...], R.sinf[...])
+        for p in range(SQ):
+            R.sb[p, :, pl.ds(0, 128)] = dq[TOK * p : TOK * (p + 1)].astype(BF16)
+        qs = pl.ds(0, 128)
+        bc = [L.copy(R.sb.at[p, :, qs], R.rx.at[s, :, qs], (d, p)) for p in L.seq_peers]
+        R.rx[s] = R.sb[s]
+        tick(ticks.get(4, ()))
+        for c in bc:
+            c.wait_recv()
+        for k in range(1, SQ):
+            c = back(L.seq_peers[k - 1], base + k)
+            c.wait_recv()
+            c.wait_send()
+        tick(ticks.get(5, ()))
+        unpack_pairs(R.rx, R.tb)
+        for c in (1 - L.x, L.x):
+            a = R.tb[chip(c)]
+            for t in range(3):
+                cs = pl.ds(256 * t, 256)
+                part[chip(c), cs] = mm_t(a, wq[cs])
+        L.settle()
+        c_other = reduce_chip("a", 1)
+        c_own = reduce_chip("a", 0)
+        c_cross = reduce_cross("a", c_other)
+        grad_of("qkv", x, R.tb)
+        if l == 1:
+            reload.append(local(R.st4, x))
+        tick(ticks.get(6, ()))
+        R.gres[...] = R.gres[...] + reduce_end("a", c_own, c_cross)
+        L.settle()
+        for c in reload:
+            c.wait()
+
+    L.settle_slow()
+    backward(1, TICKS[0])
+    lone_end(0, lone_out, R.hres[pl.ds(0, TOK)], R.out)
+    backward(0, TICKS[1])
+    lone_in = lone_begin(1, R.gres[pl.ds(TOK, PART)])
+    vcp = L.copy(R.va, R.vy, L.yp)
+    vcp.wait_recv()
+    R.vb[...] = R.va[...] + R.vy[...]
+    vzc = [L.copy(R.vb, R.vz3.at[k], L.zdev[k]) for k in range(ZS - 1)]
+    tick(TICKS[2][0])
+    for c in vzc:
+        c.wait_recv()
+    R.vc[...] = R.vb[...] + R.vz3[0] + R.vz3[1] + R.vz3[2]
+    vsc = L.copy(R.vc, R.vs, (L.sib, s))
+    lone_end(1, lone_in, R.gres[pl.ds(0, TOK)], R.gin)
+    tick(TICKS[2][1])
+    vsc.wait_recv()
+    R.vd[...] = R.vc[...] + R.vs[...]
+    vxc = L.copy(R.vd, R.vx, (L.xp, s))
+    tick(TICKS[2][2])
+    vxc.wait_recv()
+    R.vsum[...] = R.vd[...] + R.vx[...]
+    L.settle()
+    L.settle_slow()
+    for total in sums:
+        total.settle()
+
+
+LATER = ["g1", "G1", "u1", "U1"]
+TICKS = [
+    {
+        5: [
+            "g1", "G1", "u1", "U1", "d1", "D1",
+        ],
+        6: [
+            "o1",
+        ],
+    },
+    {
+        0: [
+            "d1", "D1",
+        ],
+        1: [
+            "g1", "G1", "u1", "U1",
+        ],
+        5: [
+            "g1", "G1", "u1", "U1", "d1", "D1",
+        ],
+        6: [
+            "g1", "G1", "u1", "U1", "o1", "q1", "r1",
+        ],
+        7: [
+            "o1", "q1", "r1",
+        ],
+    },
+    {
+        0: [
+            "q1", "r1", "D0", "g0", "d0",
+        ],
+        1: [
+            "u0", "G0", "D0", "g0", "d0", "g1", "G1", "o1",
+        ],
+        2: [
+            "u1", "U1", "q1", "r1", "q0", "U0", "u0", "G0", "D0", "g0", "d0", "o0", "r0", "q0", "U0", "u0", "G0", "D0",
+            "g0", "d0", "o0", "r0", "q0", "U0", "u0", "G0", "D0", "g0", "d0", "o0", "r0", "q0", "U0", "u0", "G0", "D0",
+            "g0", "d0", "o0", "r0", "q0", "U0", "u0", "G0", "D0", "g0", "d0", "o0", "r0", "q0", "U0", "u0", "G0", "D0",
+            "g0", "d0", "o0", "r0", "q0", "U0", "u0", "G0", "D0", "g0", "d0", "o0", "r0", "q0", "U0", "u0", "G0", "D0",
+            "g0", "d0", "o0", "r0", "q0", "U0", "u0", "G0", "D0", "g0", "d0", "o0", "r0", "q0", "U0", "u0", "G0", "o0",
+            "r0", "q0", "U0", "o0", "r0", "d1", "D1", "g1", "G1", "u1", "U1", "o1", "q1", "r1",
+        ],
+    },
+]
+
+
+def rotary():
+    half = HEAD // 2
+    freqs = 1000.0 ** (-(np.arange(half) * 2.0 / HEAD))
+    angles = np.arange(LEN)[:, None] * freqs[None, :]
+    co, si = np.cos(angles), np.sin(angles)
+    table = np.concatenate([co] * 4, axis=1), np.concatenate([-si, si, -si, si], axis=1)
+    return [jnp.asarray(t, F32) for t in table]
+
+
+def shared_device(inputs, cotangent, live, *weights):
+    sets = (weights[:9], weights[9:])
+    d = lax.axis_index("dp")
+    cosf, sinf = rotary()
+    norms = jnp.concatenate([jnp.pad(sets[i][j].astype(F32), (0, 64)) for i in range(2) for j in (2, 3, 7, 8)]).reshape(8, 256)
+    flags = jnp.broadcast_to(live.astype(F32), (2, 256))
+    aux = jnp.concatenate([norms, flags, jnp.zeros((6, 256), F32)], axis=0)
+    args = [inputs[:, 0], cotangent[:, 0], aux]
+    for i in range(2):
+        args += [sets[i][0], sets[i][4], sets[i][5], sets[i][1], sets[i][6]]
+    args += [cosf, sinf]
+    outs = OUTS + OUTS_ANY
+    res = pl.pallas_call(
+        whole_kernel,
+        name="layers",
+        out_shape=[jax.ShapeDtypeStruct(*o) for _, o in outs],
+        in_specs=[pl.BlockSpec(memory_space=pl.ANY if n in INS_ANY else pltpu.VMEM) for n in INS],
+        out_specs=[pl.BlockSpec(memory_space=pltpu.VMEM)] * len(OUTS) + [pl.BlockSpec(memory_space=pl.ANY)] * len(OUTS_ANY),
+        scratch_shapes=[pltpu.VMEM(*o) for _, o in SCRATCH]
+        + [
+            pltpu.SemaphoreType.DMA((SEMS,)),
+            pltpu.SemaphoreType.DMA((SEMS,)),
+            pltpu.SemaphoreType.DMA((64,)),
+        ],
+        cost_estimate=pl.CostEstimate(flops=4 * 10**10, bytes_accessed=5 * 10**7, transcendentals=10**7),
+        compiler_params=pltpu.CompilerParams(collective_id=1, has_side_effects=True, vmem_limit_bytes=VMEM_LIMIT),
+    )(*args)
+    grads = pl.pallas_call(
+        widen_kernel,
+        name="widen",
+        out_shape=[jax.ShapeDtypeStruct(*o) for o in GRADS + GRADS + [((2, TOK, D), BF16)] * 2],
+        in_specs=[pl.BlockSpec(memory_space=pl.ANY)] * 4,
+        out_specs=[pl.BlockSpec(memory_space=pl.ANY)] * 12,
+        scratch_shapes=[
+            pltpu.VMEM((2, BLOCKS, QR, D), BF16),
+            pltpu.VMEM((STAGES, QR, D), F32),
+            pltpu.SemaphoreType.DMA((12,)),
+            pltpu.SemaphoreType.DMA((STAGES,)),
+        ],
+        cost_estimate=pl.CostEstimate(flops=10**7, bytes_accessed=3 * 10**7, transcendentals=0),
+        compiler_params=pltpu.CompilerParams(vmem_limit_bytes=40 * 2**20),
+    )(res[3], res[4], res[0], res[1])
+    vsum = lax.dynamic_slice_in_dim(res[2], d * QR, QR, 1)
+    out = [grads[10][:, None], grads[11][:, None]]
+    for i in range(2):
+        g_qkv, g_out, g_gate, g_up, g_down = grads[5 * i : 5 * i + 5]
+        v = vsum[4 * i : 4 * i + 4]
+        out += [g_qkv, g_out, v[0], v[1], g_gate, g_up, g_down, v[2], v[3]]
+    return tuple(out)
+
+
+def fits(mesh):
+    return mesh.shape["dp"] == DP and mesh.shape["seq"] == SQ
 
 
 def as_sent(array):
@@ -294,8 +1562,13 @@
 
 
 def solution(mesh):
+    def device(inputs, cotangent, *rest):
+        if fits(mesh) and inputs.shape == (2, 1, TOK, D):
+            return shared_device(inputs, cotangent, *rest)
+        return per_device(inputs, cotangent, *rest)
+
     return jax.shard_map(
-        per_device,
+        device,
         mesh=mesh,
         in_specs=(
             P(None, "dp", "seq", None),

time: 2100 us -> 517 us (0.25)
  waiting for transfers between devices: 1610 us -> 0 us
  Pallas kernels: 0 us -> 489 us
  matrix products: 219 us -> 0 us
  local copies, waits for them, and re-layouts: 113 us -> 15.7 us
  other arithmetic: 78.2 us -> 1.34 us
  blocking collectives: 46.3 us -> 0 us
    all_gather x18 -> x0, waiting for transfers between devices: 561 us -> none  [the longest x10 283 us: per_device(): full = lax.all_gather(as_sent(local_sets[index]), 'dp', axis=0, tiled=True)]
    pallas_call x0 -> x2, Pallas kernels: none -> 489 us  [the longest x1 480 us: shared_device(): pl.pallas_call(whole_kernel, name='layers', out_shape=[jax.ShapeDtypeStru...]
    unnamed x46 -> x0, waiting for transfers between devices: 405 us -> none
    reduce_scatter x9 -> x0, waiting for transfers between devices: 393 us -> none  [per_device(): lax.psum_scatter(as_sent(totals[index]), 'dp', scatter_dimension=0, tiled...]
    psum x1 -> x0, waiting for transfers between devices: 248 us -> none  [per_device(): lax.psum(as_sent(shares), 'seq')]
    dot_general x84 -> x0, matrix products: 219 us -> none  [the longest x20 48.6 us: dot_first(): lax.dot_general(left, right, (((0,), (0,)), ((), ())), preferred_element_...]
    unnamed x608 -> x15, local copies, waits for them, and re-layouts: 92.8 us -> 8.22 us
    convert_element_type x41 -> x0, other arithmetic: 43.3 us -> none  [the longest x17 22.6 us: per_device(): part.astype(jnp.float32)]
  transfers between devices with their start and end apart: 37 -> 0, of which waited for: 36 -> 0; matrix products, arithmetic and copies ran while one was open for 15% -> 0% of each run, Pallas kernels for 0% -> 0%
where the time goes in v2:
time: 517 us; the launch traced here: 507 us
  Pallas kernels  489 us (95%)
  local copies, waits for them, and re-layouts  15.7 us (3%)
    pallas_call x1, Pallas kernels, shared_device(): pl.pallas_call(whole_kernel, name='layers', out_shape=[jax.ShapeDtypeStru...  480 us

profile of v2, /device:TPU:10, one launch (start us, length us, event | category | flops | bytes accessed | tf_op | source)
XLA Modules:
  0.0 506.7 jit_solution(4646310319823902250)
XLA Ops:
  0.7 0.7 convert_bitcast_fusion
  1.3 0.1 pad.42.clone
  1.4 0.7 pad.33
  2.1 0.7 pad.34
  2.7 0.7 pad.35
  3.4 0.7 pad.36
  4.0 0.7 pad.37
  4.7 0.7 pad.38
  5.4 0.7 pad.39
  6.0 0.7 pad.40
  6.7 0.1 pad.43.clone
  6.8 0.2 dynamic-update-slice
  6.9 0.2 dynamic-update-slice.1
  7.2 0.2 dynamic-update-slice.2
  7.4 0.2 dynamic-update-slice.3
  7.6 0.2 dynamic-update-slice.4
  7.8 0.2 dynamic-update-slice.5
  8.0 0.2 dynamic-update-slice.6
  8.1 0.2 dynamic-update-slice.7
  8.4 0.7 maximum_maximum_fusion.refs_2_
  9.0 479.7 %layers.1 = (bf16[2,128,768]{2,1,0:T(8,128)(2,1)}, bf16[2,128,768]{2,1,0:T(8,128)(2,1)}, f32[8,768]{1,0:T(8,128)}, bf16[17,192,768]{2,1,0:T(8,128)(2,1)}, bf16[1...) custom-call(bf16[2,128,768]{2,1,0:T(8,128)(2,1)} %bitcast.26, ...), custom_call_target="tpu_custom_call" | custom-call | flops 40000000000 | bytes 50000000 | tf_op jit(solution)/shard_map/layers/pallas_call | solution.py:1234
  488.8 1.9 fusion
  490.6 0.0 copy-start
  490.6 2.4 copy-done
  493.0 0.0 copy-start.1
  493.0 2.4 copy-done.1
  495.5 0.0 copy-start.2
  495.5 1.0 copy-done.2
  496.5 0.0 copy-start.3
  496.5 1.0 copy-done.3
  497.5 8.8 %widen.1 = (f32[192,2304]{1,0:T(8,128)}, f32[192,768]{1,0:T(8,128)}, f32[192,3072]{1,0:T(8,128)}, f32[192,3072]{1,0:T(8,128)}, f32[768,768]{1,0:T(8,128)}, /*ind...) custom-call(bf16[17,192,768]{2,1,0:T(8,128)(2,1)S(1)} %copy-done, ...), custom_call_target="tpu_custom_call" | custom-call | flops 10000000 | bytes 30000000 | tf_op jit(solution)/shard_map/widen/pallas_call | solution.py:1249
  (3 shorter events, 0.0 us)
Async XLA Ops:
  490.6 2.4 copy-start
  493.0 2.4 copy-start.1
  495.5 1.0 copy-start.2
  496.5 1.0 copy-start.3

commit v3 on v2

--- a/solution.py
+++ b/solution.py
@@ -1164,49 +1164,25 @@
         total.settle()
 
 
-LATER = ["g1", "G1", "u1", "U1"]
+def of(names, layer):
+    return [n + str(layer) for n in names]
+
+
+def staggered(chunks, beats=40, depth=11):
+    return [[c for c, begin in reversed(chunks) if 0 <= t - begin < depth] for t in range(beats)]
+
+
+FEED = "gGuU"
+LATER = of(FEED, 1) + of(FEED, 0)
+LAST = staggered(list(zip(of("dgDGuUqro", 0), (0, 0, 0, 1, 1, 2, 2, 3, 3))))
+LAST[0] = of("oqr", 1) + LAST[0]
+LAST[1] = LAST[1] + of(FEED, 1)
+LAST[2] = of("oqr", 1) + LAST[2]
+LAST[4] = of("oqr", 1) + LAST[4]
 TICKS = [
-    {
-        5: [
-            "g1", "G1", "u1", "U1", "d1", "D1",
-        ],
-        6: [
-            "o1",
-        ],
-    },
-    {
-        0: [
-            "d1", "D1",
-        ],
-        1: [
-            "g1", "G1", "u1", "U1",
-        ],
-        5: [
-            "g1", "G1", "u1", "U1", "d1", "D1",
-        ],
-        6: [
-            "g1", "G1", "u1", "U1", "o1", "q1", "r1",
-        ],
-        7: [
-            "o1", "q1", "r1",
-        ],
-    },
-    {
-        0: [
-            "q1", "r1", "D0", "g0", "d0",
-        ],
-        1: [
-            "u0", "G0", "D0", "g0", "d0", "g1", "G1", "o1",
-        ],
-        2: [
-            "u1", "U1", "q1", "r1", "q0", "U0", "u0", "G0", "D0", "g0", "d0", "o0", "r0", "q0", "U0", "u0", "G0", "D0",
-            "g0", "d0", "o0", "r0", "q0", "U0", "u0", "G0", "D0", "g0", "d0", "o0", "r0", "q0", "U0", "u0", "G0", "D0",
-            "g0", "d0", "o0", "r0", "q0", "U0", "u0", "G0", "D0", "g0", "d0", "o0", "r0", "q0", "U0", "u0", "G0", "D0",
-            "g0", "d0", "o0", "r0", "q0", "U0", "u0", "G0", "D0", "g0", "d0", "o0", "r0", "q0", "U0", "u0", "G0", "D0",
-            "g0", "d0", "o0", "r0", "q0", "U0", "u0", "G0", "D0", "g0", "d0", "o0", "r0", "q0", "U0", "u0", "G0", "o0",
-            "r0", "q0", "U0", "o0", "r0", "d1", "D1", "g1", "G1", "u1", "U1", "o1", "q1", "r1",
-        ],
-    },
+    {5: of("gGuUdD", 1), 6: of("o", 1)},
+    {0: of("dD", 1), 1: of(FEED, 1), 7: of(FEED, 1), 5: of(FEED, 0) + of("gGuUdDoqr", 1), 6: []},
+    {0: LAST[0], 1: LAST[1], 2: sum(LAST[2:], []) + of("dDgGuUoqr", 1)},
 ]
 
 

time: 517 us -> 505 us (0.977)
  Pallas kernels: 489 us -> 479 us
    pallas_call x1, Pallas kernels: 480 us -> 470 us  [shared_device(): pl.pallas_call(whole_kernel, name='layers', out_shape=[jax.ShapeDtypeStru...]
where the time goes in v3:
time: 505 us; the launch traced here: 497 us
  Pallas kernels  479 us (95%)
  local copies, waits for them, and re-layouts  15.7 us (3%)
    pallas_call x1, Pallas kernels, shared_device(): pl.pallas_call(whole_kernel, name='layers', out_shape=[jax.ShapeDtypeStru...  470 us

profile of v3, /device:TPU:10, one launch (start us, length us, event | category | flops | bytes accessed | tf_op | source)
XLA Modules:
  0.0 496.8 jit_solution(18106357396053540500)
XLA Ops:
  0.7 0.7 convert_bitcast_fusion
  1.3 0.1 pad.42.clone
  1.4 0.7 pad.33
  2.1 0.7 pad.34
  2.7 0.7 pad.35
  3.4 0.7 pad.36
  4.0 0.7 pad.37
  4.7 0.7 pad.38
  5.4 0.7 pad.39
  6.0 0.7 pad.40
  6.7 0.1 pad.43.clone
  6.8 0.2 dynamic-update-slice
  6.9 0.2 dynamic-update-slice.1
  7.2 0.2 dynamic-update-slice.2
  7.4 0.2 dynamic-update-slice.3
  7.6 0.2 dynamic-update-slice.4
  7.8 0.2 dynamic-update-slice.5
  8.0 0.2 dynamic-update-slice.6
  8.1 0.2 dynamic-update-slice.7
  8.4 0.7 maximum_maximum_fusion.refs_2_
  9.0 469.8 %layers.1 = (bf16[2,128,768]{2,1,0:T(8,128)(2,1)}, bf16[2,128,768]{2,1,0:T(8,128)(2,1)}, f32[8,768]{1,0:T(8,128)}, bf16[17,192,768]{2,1,0:T(8,128)(2,1)}, bf16[1...) custom-call(bf16[2,128,768]{2,1,0:T(8,128)(2,1)} %bitcast.26, ...), custom_call_target="tpu_custom_call" | custom-call | flops 40000000000 | bytes 50000000 | tf_op jit(solution)/shard_map/layers/pallas_call | solution.py:1210
  478.8 1.9 fusion
  480.7 0.0 copy-start
  480.7 2.4 copy-done
  483.1 0.0 copy-start.1
  483.1 2.4 copy-done.1
  485.5 0.0 copy-start.2
  485.5 1.0 copy-done.2
  486.5 0.0 copy-start.3
  486.5 1.0 copy-done.3
  487.5 8.8 %widen.1 = (f32[192,2304]{1,0:T(8,128)}, f32[192,768]{1,0:T(8,128)}, f32[192,3072]{1,0:T(8,128)}, f32[192,3072]{1,0:T(8,128)}, f32[768,768]{1,0:T(8,128)}, /*ind...) custom-call(bf16[17,192,768]{2,1,0:T(8,128)(2,1)S(1)} %copy-done, ...), custom_call_target="tpu_custom_call" | custom-call | flops 10000000 | bytes 30000000 | tf_op jit(solution)/shard_map/widen/pallas_call | solution.py:1225
  (3 shorter events, 0.0 us)
Async XLA Ops:
  480.7 2.4 copy-start
  483.1 2.4 copy-start.1
  485.5 1.0 copy-start.2
  486.5 1.0 copy-start.3
